TPU v7x, 32 devices: a whole 2x2x4 slice. The times are simulated.
32 devices in a mesh: dp: 8 (over z, x), sy: 2 (over y), sx: 2 (over core).
Axes of the slice: x: 2, y: 2, z: 4, core: 2. Of those that a mesh axis runs over, the one named last changes fastest.
Arguments:
- features: bfloat16 [8, 16, 32, 640], P('dp', 'sy', 'sx'), may hold values from -6 to 6
- bucket_ids: int32 [8], P('dp'), may hold values from 0 to 7
- bucket_sizes: int32 [8, 2], replicated, may hold values from 8 to 32, as said below
- conv_weight: bfloat16 [5760, 640], replicated, may hold values from -0.078125 to 0.078125
- norm_gain: float32 [640], replicated, may hold values from 0.25 to 1.75
- query_weight: bfloat16 [640, 640], replicated, may hold values from -0.25 to 0.25
- key_weight: bfloat16 [640, 640], replicated, may hold values from -0.25 to 0.25
- value_weight: bfloat16 [640, 640], replicated, may hold values from -0.25 to 0.25
- out_weight: bfloat16 [640, 640], replicated, may hold values from -0.25 to 0.25
- out_grad: bfloat16 [8, 16, 32, 640], P('dp', 'sy', 'sx'), may hold values from -6 to 6
Outputs:
- block_out: bfloat16 [8, 16, 32, 640], P('dp', 'sy', 'sx')
- grad_conv: float32 [5760, 640], P('dp', ('sy', 'sx'))
- grad_query: float32 [640, 640], P('dp', ('sy', 'sx'))
- grad_key: float32 [640, 640], P('dp', ('sy', 'sx'))
- grad_value: float32 [640, 640], P('dp', ('sy', 'sx'))
- grad_out: float32 [640, 640], P('dp', ('sy', 'sx'))
Inputs may be any that keep to these rules, and one draw needn't show every extreme that they name: Each row of bucket_sizes holds a bucket's latent rows, from 8 to 16, and columns, from 16 to 32; bucket 0 is the full 16 x 32 grid and bucket 1 is 8 x 16.
All inputs are finite; a program needn't handle non-finite values.
Results may differ from a plain program's by a relative error of at most 0.013.
Values may be sent and summed in bfloat16 or wider, within the bound.
A program may use at most 192 MiB of HBM per device.

v0:
```python
import jax
import jax.numpy as jnp
from jax import lax
from jax.sharding import PartitionSpec as P

HEADS = 10


def extended(block, sides, width):
    for axis, dim in sides:
        count = lax.axis_size(axis)
        forward = [(i, i + 1) for i in range(count - 1)]
        backward = [(target, source) for source, target in forward]
        low = lax.ppermute(
            lax.slice_in_dim(block, block.shape[dim] - width, None, axis=dim), axis, forward
        )
        high = lax.ppermute(lax.slice_in_dim(block, 0, width, axis=dim), axis, backward)
        block = jnp.concatenate([low, block, high], axis=dim)
    return block


def layer_norm(hidden, gain):
    mean = jnp.mean(hidden, axis=-1, keepdims=True)
    centred = hidden - mean
    spread = jnp.mean(centred * centred, axis=-1, keepdims=True)
    return centred * lax.rsqrt(spread + 1e-05) * gain


def patch_rows(padded, rows, cols):
    taps = [padded[dy : dy + rows, dx : dx + cols, :] for dy in range(3) for dx in range(3)]
    return jnp.concatenate(taps, axis=-1).reshape(rows * cols, -1)


def masked_scores(query, keys, key_valid, start, width, scale):
    scores = (
        jnp.dot(
            query[:, start : start + width],
            keys[:, start : start + width].T,
            preferred_element_type=jnp.float32,
        )
        * scale
    )
    return jnp.where(key_valid[None, :], scores, -1e30)


def head_probs(query, keys, key_valid, start, width, scale):
    return jax.nn.softmax(masked_scores(query, keys, key_valid, start, width, scale), axis=-1)


def attend(query, keys, values, key_valid, heads):
    width = query.shape[1] // heads
    scale = width ** (-0.5)
    parts = []
    for head in range(heads):
        start = head * width
        probs = head_probs(query, keys, key_valid, start, width, scale)
        parts.append(
            jnp.dot(
                probs.astype(jnp.bfloat16),
                values[:, start : start + width],
                preferred_element_type=jnp.float32,
            ).astype(jnp.bfloat16)
        )
    return jnp.concatenate(parts, axis=-1)


def query_side(query, keys, values, key_valid, grad_context, heads):
    width = query.shape[1] // heads
    scale = width ** (-0.5)
    dq_parts, lse_parts, delta_parts = ([], [], [])
    for head in range(heads):
        start = head * width
        scores = masked_scores(query, keys, key_valid, start, width, scale)
        top = jnp.max(scores, axis=-1, keepdims=True)
        expo = jnp.exp(scores - top)
        total = jnp.sum(expo, axis=-1, keepdims=True)
        probs = expo / total
        grad_slice = grad_context[:, start : start + width]
        dprob = jnp.dot(
            grad_slice, values[:, start : start + width].T, preferred_element_type=jnp.float32
        )
        delta = jnp.sum(probs * dprob, axis=-1, keepdims=True)
        dscore = (probs * (dprob - delta) * scale).astype(jnp.bfloat16)
        dq_parts.append(
            jnp.dot(dscore, keys[:, start : start + width], preferred_element_type=jnp.float32)
        )
        lse_parts.append(top + jnp.log(total))
        delta_parts.append(delta)
    return (
        jnp.concatenate(dq_parts, axis=-1),
        jnp.concatenate(lse_parts, axis=-1),
        jnp.concatenate(delta_parts, axis=-1),
    )


def key_side(query_all, grad_all, lse_all, delta_all, keys, values, key_valid, heads):
    width = keys.shape[1] // heads
    scale = width ** (-0.5)
    dk_parts, dv_parts = ([], [])
    for head in range(heads):
        start = head * width
        scores = masked_scores(query_all, keys, key_valid, start, width, scale)
        probs = jnp.exp(scores - lse_all[:, head : head + 1])
        probs_b = probs.astype(jnp.bfloat16)
        grad_slice = grad_all[:, start : start + width]
        dprob = jnp.dot(
            grad_slice, values[:, start : start + width].T, preferred_element_type=jnp.float32
        )
        dscore = (probs * (dprob - delta_all[:, head : head + 1]) * scale).astype(jnp.bfloat16)
        dk_parts.append(
            jnp.dot(
                dscore.T, query_all[:, start : start + width], preferred_element_type=jnp.float32
            )
        )
        dv_parts.append(jnp.dot(probs_b.T, grad_slice, preferred_element_type=jnp.float32))
    return (jnp.concatenate(dk_parts, axis=-1), jnp.concatenate(dv_parts, axis=-1))


def body(
    features,
    bucket_ids,
    bucket_sizes,
    conv_weight,
    norm_gain,
    query_weight,
    key_weight,
    value_weight,
    out_weight,
    out_grad,
):
    rows_dev = features.shape[1]
    cols_dev = features.shape[2]
    width = features.shape[3]
    count_y = lax.axis_size("sy")
    count_x = lax.axis_size("sx")
    chosen = jnp.arange(bucket_sizes.shape[0], dtype=jnp.int32) == bucket_ids[0]
    height = jnp.sum(jnp.where(chosen, bucket_sizes[:, 0], 0))
    breadth = jnp.sum(jnp.where(chosen, bucket_sizes[:, 1], 0))
    local_rows = lax.axis_index("sy") * rows_dev + jnp.arange(rows_dev, dtype=jnp.int32)
    local_cols = lax.axis_index("sx") * cols_dev + jnp.arange(cols_dev, dtype=jnp.int32)
    valid = (local_rows[:, None] < height) & (local_cols[None, :] < breadth)
    valid_flat = valid.reshape(-1, 1).astype(jnp.float32)
    members = jnp.arange(count_y * count_x, dtype=jnp.int32)
    key_rows = (members // count_x)[:, None, None] * rows_dev + jnp.arange(
        rows_dev, dtype=jnp.int32
    )[None, :, None]
    key_cols = (members % count_x)[:, None, None] * cols_dev + jnp.arange(
        cols_dev, dtype=jnp.int32
    )[None, None, :]
    key_valid = ((key_rows < height) & (key_cols < breadth)).reshape(-1)
    xin = (features[0].astype(jnp.float32) * valid[:, :, None].astype(jnp.float32)).astype(
        jnp.bfloat16
    )
    padded = extended(xin, (("sy", 0), ("sx", 1)), 1)
    patches = patch_rows(padded, rows_dev, cols_dev)
    pre = jnp.dot(patches, conv_weight, preferred_element_type=jnp.float32)
    hidden = (valid_flat * (xin.reshape(-1, width).astype(jnp.float32) + jax.nn.silu(pre))).astype(
        jnp.bfloat16
    )
    hidden_f = hidden.astype(jnp.float32)
    normed_f, pullback = jax.vjp(lambda value: layer_norm(value, norm_gain), hidden_f)
    normed = normed_f.astype(jnp.bfloat16)
    query = jnp.dot(normed, query_weight, preferred_element_type=jnp.float32).astype(jnp.bfloat16)
    keys = jnp.dot(normed, key_weight, preferred_element_type=jnp.float32).astype(jnp.bfloat16)
    values = jnp.dot(normed, value_weight, preferred_element_type=jnp.float32).astype(jnp.bfloat16)
    keys_all, values_all = (
        lax.all_gather(keys, ("sy", "sx"), axis=0, tiled=True),
        lax.all_gather(values, ("sy", "sx"), axis=0, tiled=True),
    )
    context = attend(query, keys_all, values_all, key_valid, HEADS)
    block = (
        valid_flat * (hidden_f + jnp.dot(context, out_weight, preferred_element_type=jnp.float32))
    ).astype(jnp.bfloat16)
    grad_b = (out_grad[0].reshape(-1, width).astype(jnp.float32) * valid_flat).astype(jnp.bfloat16)
    grad_wo = jnp.dot(context.T, grad_b, preferred_element_type=jnp.float32)
    grad_context = jnp.dot(grad_b, out_weight.T, preferred_element_type=jnp.float32).astype(
        jnp.bfloat16
    )
    dquery, row_lse, row_delta = query_side(
        query, keys_all, values_all, key_valid, grad_context, HEADS
    )
    query_all, grad_all = (
        lax.all_gather(query, ("sy", "sx"), axis=0, tiled=True),
        lax.all_gather(grad_context, ("sy", "sx"), axis=0, tiled=True),
    )
    lse_all, delta_all = (
        lax.all_gather(row_lse, ("sy", "sx"), axis=0, tiled=True),
        lax.all_gather(row_delta, ("sy", "sx"), axis=0, tiled=True),
    )
    dkey, dvalue = key_side(
        query_all, grad_all, lse_all, delta_all, keys, values, valid.reshape(-1), HEADS
    )
    dquery = dquery.astype(jnp.bfloat16)
    dkey = dkey.astype(jnp.bfloat16)
    dvalue = dvalue.astype(jnp.bfloat16)
    grad_wq = jnp.dot(normed.T, dquery, preferred_element_type=jnp.float32)
    grad_wk = jnp.dot(normed.T, dkey, preferred_element_type=jnp.float32)
    grad_wv = jnp.dot(normed.T, dvalue, preferred_element_type=jnp.float32)
    dnormed = jnp.dot(dquery, query_weight.T, preferred_element_type=jnp.float32)
    dnormed = dnormed + jnp.dot(dkey, key_weight.T, preferred_element_type=jnp.float32)
    dnormed = dnormed + jnp.dot(dvalue, value_weight.T, preferred_element_type=jnp.float32)
    dhidden = grad_b.astype(jnp.float32) + pullback(dnormed)[0]
    sig = jax.nn.sigmoid(pre)
    dpre = (valid_flat * dhidden * sig * (1.0 + pre * (1.0 - sig))).astype(jnp.bfloat16)
    grad_cv = jnp.dot(patches.T, dpre, preferred_element_type=jnp.float32)
    summed = (
        lax.psum_scatter(grad_cv, "dp", scatter_dimension=0, tiled=True),
        lax.psum_scatter(grad_wq, "dp", scatter_dimension=0, tiled=True),
        lax.psum_scatter(grad_wk, "dp", scatter_dimension=0, tiled=True),
        lax.psum_scatter(grad_wv, "dp", scatter_dimension=0, tiled=True),
        lax.psum_scatter(grad_wo, "dp", scatter_dimension=0, tiled=True),
    )
    summed = (
        lax.psum_scatter(summed[0], ("sy", "sx"), scatter_dimension=1, tiled=True),
        lax.psum_scatter(summed[1], ("sy", "sx"), scatter_dimension=1, tiled=True),
        lax.psum_scatter(summed[2], ("sy", "sx"), scatter_dimension=1, tiled=True),
        lax.psum_scatter(summed[3], ("sy", "sx"), scatter_dimension=1, tiled=True),
        lax.psum_scatter(summed[4], ("sy", "sx"), scatter_dimension=1, tiled=True),
    )
    block_out = block.reshape(1, rows_dev, cols_dev, width)
    return (block_out, summed[0], summed[1], summed[2], summed[3], summed[4])


def solution(mesh):
    placed = (
        P("dp", "sy", "sx", None),
        P("dp"),
        P(),
        P(),
        P(),
        P(),
        P(),
        P(),
        P(),
        P("dp", "sy", "sx", None),
    )
    return jax.shard_map(
        body,
        mesh=mesh,
        in_specs=placed,
        out_specs=(
            P("dp", "sy", "sx", None),
            P("dp", ("sy", "sx")),
            P("dp", ("sy", "sx")),
            P("dp", ("sy", "sx")),
            P("dp", ("sy", "sx")),
            P("dp", ("sy", "sx")),
        ),
        check_vma=False,
    )
```

profile of v0, /device:TPU:24, one launch (start us, length us, event | category | flops | bytes accessed | tf_op | source)
XLA Modules:
  0.0 751.4 jit_solution(12032524503318369310)
XLA Ops:
  11.8 3.4 collective-permute-start
  22.3 3.0 collective-permute-start.2
  27.2 5.3 convert_reduce_fusion
  34.0 8.5 %all_gather.20 = bf16[512,640]{1,0:T(8,128)(2,1)} all-gather(bf16[128,640]{1,0:T(8,128)(2,1)S(1)} %convolution_convert_fusion.3), channel_id=1, replica_groups=mesh['dp'=8,'sy'=2,'sx'=2] {'sy','sx'}, dimensions={0}, use_global_device_ids=true | all-gather | bytes 819200 | tf_op jit(solution)/shard_map/all_gather | solution.py:183
  42.5 8.1 %all_gather.18 = bf16[512,640]{1,0:T(8,128)(2,1)S(1)} all-gather(bf16[128,640]{1,0:T(8,128)(2,1)S(1)} %convolution_convert_fusion.2), channel_id=1, replica_groups=mesh['dp'=8,'sy'=2,'sx'=2] {'sy','sx'}, dimensions={0}, use_global_device_ids=true | all-gather | bytes 819200 | tf_op jit(solution)/shard_map/all_gather | solution.py:167
  52.4 8.5 %all_gather.22 = bf16[512,640]{1,0:T(8,128)(2,1)} all-gather(bf16[128,640]{1,0:T(8,128)(2,1)S(1)} %convolution_convert_fusion), channel_id=1, replica_groups=mesh['dp'=8,'sy'=2,'sx'=2] {'sy','sx'}, dimensions={0}, use_global_device_ids=true | all-gather | bytes 819200 | tf_op jit(solution)/shard_map/all_gather | solution.py:184
  60.8 8.0 %all_gather.19 = bf16[512,640]{1,0:T(8,128)(2,1)S(1)} all-gather(bf16[128,640]{1,0:T(8,128)(2,1)S(1)} %convolution_convert_fusion.1), channel_id=1, replica_groups=mesh['dp'=8,'sy'=2,'sx'=2] {'sy','sx'}, dimensions={0}, use_global_device_ids=true | all-gather | bytes 819200 | tf_op jit(solution)/shard_map/all_gather | solution.py:168
  88.6 2.6 concatenate.52
  91.2 5.7 all_gather.21
  112.2 2.6 multiply_reduce_fusion.8
  114.9 2.6 concatenate.53
  117.4 5.4 all_gather.23
  144.1 2.6 fusion.429
  168.4 7.5 fusion.164
  177.8 64.3 %reduce-scatter.25.cloned.1.call-done = f32[80,640]{1,0:T(8,128)} async-done(((f32[640,640]{1,0:T(8,128)}), f32[80,640]{1,0:T(8,128)}) %reduce-scatter.25.cloned.1.call-update) | async-done | bytes 204816 | tf_op jit(solution)/shard_map/reduce_scatter | solution.py:209
  244.1 65.9 %reduce-scatter.23.cloned.1.call-done = f32[80,640]{1,0:T(8,128)} async-done(((f32[640,640]{1,0:T(8,128)}), f32[80,640]{1,0:T(8,128)}) %reduce-scatter.23.cloned.1.call-update) | async-done | bytes 204816 | tf_op jit(solution)/shard_map/reduce_scatter | solution.py:208
  311.9 66.1 %reduce-scatter.29.cloned.1.call-done = f32[80,640]{1,0:T(8,128)} async-done(((f32[640,640]{1,0:T(8,128)}), f32[80,640]{1,0:T(8,128)}) %reduce-scatter.29.cloned.1.call-update) | async-done | bytes 204816 | tf_op jit(solution)/shard_map/reduce_scatter | solution.py:211
  379.9 237.5 %reduce-scatter.21.cloned.1.call-done = f32[720,640]{1,0:T(8,128)} async-done(((f32[5760,640]{1,0:T(8,128)}), f32[720,640]{1,0:T(8,128)}) %reduce-scatter.21.cloned.1.call-update) | async-done | bytes 1843216 | tf_op jit(solution)/shard_map/reduce_scatter | solution.py:207
  617.4 2.9 copy.18
  622.4 19.2 %reduce-scatter.37.cloned.1.call-done = f32[160,80]{1,0:T(8,128)} async-done(((f32[640,80]{1,0:T(8,128)}), f32[160,80]{1,0:T(8,128)}) %reduce-scatter.37.cloned.1.call-update) | async-done | bytes 51216
  643.2 21.4 %reduce-scatter.35.cloned.1.call-done = f32[160,80]{1,0:T(8,128)} async-done(((f32[640,80]{1,0:T(8,128)}), f32[160,80]{1,0:T(8,128)}) %reduce-scatter.35.cloned.1.call-update) | async-done | bytes 51216
  666.2 21.5 %reduce-scatter.33.cloned.1.call-done = f32[160,80]{1,0:T(8,128)} async-done(((f32[640,80]{1,0:T(8,128)}), f32[160,80]{1,0:T(8,128)}) %reduce-scatter.33.cloned.1.call-update) | async-done | bytes 51216
  689.3 21.4 %reduce-scatter.39.cloned.1.call-done = f32[160,80]{1,0:T(8,128)} async-done(((f32[640,80]{1,0:T(8,128)}), f32[160,80]{1,0:T(8,128)}) %reduce-scatter.39.cloned.1.call-update) | async-done | bytes 51216
  712.3 32.2 %reduce-scatter.31.cloned.1.call-done = f32[160,720]{1,0:T(8,128)} async-done(((f32[640,720]{1,0:T(8,128)}), f32[160,720]{1,0:T(8,128)}) %reduce-scatter.31.cloned.1.call-update) | async-done | bytes 460816
  (439 shorter events, 108.6 us)
Async XLA Ops:
  7.2 44.4 %copy-start = (bf16[640,640]{1,0:T(8,128)(2,1)S(1)}, bf16[640,640]{1,0:T(8,128)(2,1)}, u32[]{:S(2)}) copy-start(bf16[640,640]{1,0:T(8,128)(2,1)} %param.17) | copy-start | bytes 2457604
  7.2 19.2 %copy-start.8 = (bf16[1,8,16,640]{3,2,1,0:T(8,128)(2,1)S(1)}, bf16[1,8,16,640]{3,2,1,0:T(8,128)(2,1)}, u32[]{:S(2)}) copy-start(bf16[1,8,16,640]{3,2,1,0:T(8,128)(2,1)} %param.10) | copy-start | bytes 491524
  7.2 168.7 %reduce-scatter.27.cloned.1.call-start = ((), (), s32[]{:S(2)}) async-start(), calls=%async_computation.13 | async-start | bytes 1843200 | tf_op jit(solution)/shard_map/reduce_scatter | solution.py:210
  11.8 6.6 collective-permute-start
  15.2 5.7 collective-permute-start.1
  21.0 4.9 collective-permute-start.3
  22.3 3.9 collective-permute-start.2
  50.9 18.6 %copy-start.83 = (f32[128]{0:T(128)}, f32[128]{0:T(128)S(1)}, u32[]{:S(2)}) copy-start(f32[128]{0:T(128)S(1)} %get-tuple-element.71) | copy-start | bytes 1540
  51.2 20.0 %copy-start.10 = (f32[128,512]{1,0:T(8,128)}, f32[128,512]{1,0:T(8,128)S(1)}, u32[]{:S(2)}) copy-start(f32[128,512]{1,0:T(8,128)S(1)} %get-tuple-element.70) | copy-start | bytes 786436
  51.2 21.7 %copy-start.60 = (f32[128]{0:T(128)}, f32[128]{0:T(128)S(1)}, u32[]{:S(2)}) copy-start(f32[128]{0:T(128)S(1)} %get-tuple-element.69) | copy-start | bytes 1540
  51.6 21.9 %copy-start.13 = (f32[128,512]{1,0:T(8,128)}, f32[128,512]{1,0:T(8,128)S(1)}, u32[]{:S(2)}) copy-start(f32[128,512]{1,0:T(8,128)S(1)} %get-tuple-element.68) | copy-start | bytes 786436
  51.6 21.9 %copy-start.62 = (f32[128]{0:T(128)}, f32[128]{0:T(128)S(1)}, u32[]{:S(2)}) copy-start(f32[128]{0:T(128)S(1)} %get-tuple-element.67) | copy-start | bytes 1540
  52.0 17.0 %copy-start.43 = (bf16[128,640]{1,0:T(8,128)(2,1)}, bf16[128,640]{1,0:T(8,128)(2,1)S(1)}, u32[]{:S(2)}) copy-start(bf16[128,640]{1,0:T(8,128)(2,1)S(1)} %convolution_convert_fusion.1) | copy-start | bytes 491524
  52.4 33.2 %copy-start.40 = (bf16[128,640]{1,0:T(8,128)(2,1)}, bf16[128,640]{1,0:T(8,128)(2,1)S(1)}, u32[]{:S(2)}) copy-start(bf16[128,640]{1,0:T(8,128)(2,1)S(1)} %convolution_convert_fusion) | copy-start | bytes 491524
  68.8 16.7 %copy-start.37 = (bf16[512,640]{1,0:T(8,128)(2,1)}, bf16[512,640]{1,0:T(8,128)(2,1)S(1)}, u32[]{:S(2)}) copy-start(bf16[512,640]{1,0:T(8,128)(2,1)S(1)} %all_gather.19) | copy-start | bytes 1966084
  109.7 132.4 %reduce-scatter.25.cloned.1.call-start = ((), (), s32[]{:S(2)}) async-start(), calls=%async_computation.12 | async-start | bytes 1843200 | tf_op jit(solution)/shard_map/reduce_scatter | solution.py:209
  146.8 163.2 %reduce-scatter.23.cloned.1.call-start = ((), (), s32[]{:S(2)}) async-start(), calls=%async_computation.11 | async-start | bytes 1843200 | tf_op jit(solution)/shard_map/reduce_scatter | solution.py:208
  155.8 222.1 %reduce-scatter.29.cloned.1.call-start = ((), (), s32[]{:S(2)}) async-start(), calls=%async_computation.14 | async-start | bytes 1843200 | tf_op jit(solution)/shard_map/reduce_scatter | solution.py:211
  164.3 453.1 %reduce-scatter.21.cloned.1.call-start = ((), (), s32[]{:S(2)}) async-start(), calls=%async_computation.10 | async-start | bytes 16588800 | tf_op jit(solution)/shard_map/reduce_scatter | solution.py:207
  175.9 465.8 %reduce-scatter.37.cloned.1.call-start = ((), (), s32[]{:S(2)}) async-start(), calls=%async_computation.18 | async-start | bytes 409600
  177.8 486.8 %reduce-scatter.35.cloned.1.call-start = ((), (), s32[]{:S(2)}) async-start(), calls=%async_computation.17 | async-start | bytes 409600
  244.0 443.7 %reduce-scatter.33.cloned.1.call-start = ((), (), s32[]{:S(2)}) async-start(), calls=%async_computation.16 | async-start | bytes 409600
  311.8 398.9 %reduce-scatter.39.cloned.1.call-start = ((), (), s32[]{:S(2)}) async-start(), calls=%async_computation.19 | async-start | bytes 409600
  379.8 364.7 %reduce-scatter.31.cloned.1.call-start = ((), (), s32[]{:S(2)}) async-start(), calls=%async_computation.15 | async-start | bytes 2457600
  (125 other events, 308.6 us)
Sparse Core Ops, SparseCore 0:
  109.8 64.2 reduce-scatter.26
  177.9 64.1 reduce-scatter.24
  245.6 64.3 reduce-scatter.22
  313.7 64.2 reduce-scatter.28
  381.4 235.9 reduce-scatter.20
  619.9 21.7 reduce-scatter.36
  644.1 20.4 reduce-scatter.34
  667.3 20.4 reduce-scatter.32
  690.2 20.4 reduce-scatter.38
  713.9 30.6 reduce-scatter.30
where the time goes:
time: 754 us; the launch traced here: 751 us
  waiting for transfers between devices  552 us (73%)
  matrix products  87.1 us (12%)
  blocking collectives  44.1 us (6%)
  local copies, waits for them, and re-layouts  29.6 us (4%)
  between operations  16.7 us (2%)
  other arithmetic  11.9 us (2%)
  starting transfers between devices  9.67 us (1%)
    reduce_scatter x1, waiting for transfers between devices, body(): lax.psum_scatter(grad_cv, 'dp', scatter_dimension=0, tiled=True)  238 us
    unnamed x15, waiting for transfers between devices  116 us
    reduce_scatter x1, waiting for transfers between devices, body(): lax.psum_scatter(grad_wo, 'dp', scatter_dimension=0, tiled=True)  66.1 us
    reduce_scatter x1, waiting for transfers between devices, body(): lax.psum_scatter(grad_wq, 'dp', scatter_dimension=0, tiled=True)  65.9 us
    reduce_scatter x1, waiting for transfers between devices, body(): lax.psum_scatter(grad_wk, 'dp', scatter_dimension=0, tiled=True)  64.3 us
    unnamed x284, local copies, waits for them, and re-layouts  23.3 us
    dot_general x10, matrix products, key_side(): jnp.dot(dscore.T, query_all[:, start:start + width], preferred_element_ty...  20.7 us
    dot_general x10, matrix products, query_side(): jnp.dot(grad_slice, values[:, start:start + width].T, preferred_element_t...  17 us
  transfers between devices with their start and end apart: 14, of which 11 were waited for; matrix products, arithmetic and copies ran while one was open for 10% of the time, Pallas kernels for 0%

commit v1 on v0

v1 whole, which is shorter than its diff:
```python
import functools

import jax
import jax.numpy as jnp
from jax import lax
from jax.experimental import pallas as pl
from jax.experimental.pallas import tpu as pltpu
from jax.sharding import PartitionSpec as P

HEADS = 10
F32 = jnp.float32
BF16 = jnp.bfloat16


def layer_norm(hidden, gain):
    mean = jnp.mean(hidden, axis=-1, keepdims=True)
    centred = hidden - mean
    spread = jnp.mean(centred * centred, axis=-1, keepdims=True)
    return centred * lax.rsqrt(spread + 1e-05) * gain


def patch_rows(padded, rows, cols):
    taps = [padded[dy : dy + rows, dx : dx + cols, :] for dy in range(3) for dx in range(3)]
    return jnp.concatenate(taps, axis=-1).reshape(rows * cols, -1)


def dot_t(a, b, ca, cb):
    return lax.dot_general(a, b, (((ca,), (cb,)), ((), ())), preferred_element_type=F32)


def attention_kernel(width, valid_ref, q_ref, k_ref, v_ref, g_ref, c_ref, dq_ref, dk_ref, dv_ref):
    scale = width ** (-0.5)
    mask = valid_ref[...] > 0.0
    parts = ([], [], [], [])
    for start in range(0, q_ref.shape[1], width):
        q = q_ref[:, start : start + width]
        k = k_ref[:, start : start + width]
        v = v_ref[:, start : start + width]
        g = g_ref[:, start : start + width]
        scores = jnp.where(mask, dot_t(q, k, 1, 1) * scale, -1e30)
        expo = jnp.exp(scores - jnp.max(scores, axis=-1, keepdims=True))
        probs = expo * (1.0 / jnp.sum(expo, axis=-1, keepdims=True))
        probs_b = probs.astype(BF16)
        dprob = dot_t(g, v, 1, 1)
        delta = jnp.sum(probs * dprob, axis=-1, keepdims=True)
        dscore = (probs * (dprob - delta) * scale).astype(BF16)
        parts[0].append(dot_t(probs_b, v, 1, 0))
        parts[1].append(dot_t(dscore, k, 1, 0))
        parts[2].append(dot_t(dscore, q, 0, 0))
        parts[3].append(dot_t(probs_b, g, 0, 0))
    for ref, part in zip((c_ref, dq_ref, dk_ref, dv_ref), parts):
        ref[...] = jnp.concatenate(part, axis=-1).astype(BF16)


def attention(valid_row, query, keys, values, grads, heads):
    cells, channels = query.shape
    width = channels // heads
    block = pl.BlockSpec((cells, 2 * width), lambda i: (0, i))
    shape = jax.ShapeDtypeStruct((cells, channels), BF16)
    return pl.pallas_call(
        functools.partial(attention_kernel, width),
        grid=(heads // 2,),
        in_specs=[pl.BlockSpec((1, cells), lambda i: (0, 0))] + [block] * 4,
        out_specs=[block] * 4,
        out_shape=[shape] * 4,
        compiler_params=pltpu.CompilerParams(vmem_limit_bytes=48 * 1024 * 1024),
        cost_estimate=pl.CostEstimate(
            flops=12 * cells * cells * channels,
            bytes_accessed=16 * cells * channels,
            transcendentals=heads * cells * cells,
        ),
    )(valid_row, query, keys, values, grads)


def exchange_kernel(count, a_ref, b_ref, a_out, b_out, a_got, b_got, send_sem, recv_sem):
    me = lax.axis_index("dp")
    barrier = pltpu.get_barrier_semaphore()
    for step in range(1, count):
        pl.semaphore_signal(
            barrier,
            inc=1,
            device_id={"dp": lax.rem(me + step, count)},
            device_id_type=pl.DeviceIdType.MESH,
        )
    pl.semaphore_wait(barrier, count - 1)
    copies = []
    for which, (src, got) in enumerate(((a_ref, a_got), (b_ref, b_got))):
        for step in range(1, count):
            peer = lax.rem(me + step, count)
            copy = pltpu.make_async_remote_copy(
                src_ref=src.at[peer],
                dst_ref=got.at[step - 1],
                send_sem=send_sem.at[which, step - 1],
                recv_sem=recv_sem.at[which, step - 1],
                device_id={"dp": peer},
                device_id_type=pl.DeviceIdType.MESH,
            )
            copy.start()
            copies.append(copy)
    a_out[...] = a_ref[me].astype(F32)
    b_out[...] = b_ref[me].astype(F32)
    for index, copy in enumerate(copies):
        copy.wait_recv()
        step = index % (count - 1)
        if index < count - 1:
            a_out[...] += a_got[step].astype(F32)
        else:
            b_out[...] += b_got[step].astype(F32)
    for copy in copies:
        copy.wait_send()


def exchange(a, b):
    count = a.shape[0]
    vmem = pl.BlockSpec(memory_space=pltpu.VMEM)
    return pl.pallas_call(
        functools.partial(exchange_kernel, count),
        in_specs=[vmem, vmem],
        out_specs=[vmem, vmem],
        out_shape=[
            jax.ShapeDtypeStruct(a.shape[1:], F32),
            jax.ShapeDtypeStruct(b.shape[1:], F32),
        ],
        scratch_shapes=[
            pltpu.VMEM((count - 1,) + a.shape[1:], BF16),
            pltpu.VMEM((count - 1,) + b.shape[1:], BF16),
            pltpu.SemaphoreType.DMA((2, count - 1)),
            pltpu.SemaphoreType.DMA((2, count - 1)),
        ],
        compiler_params=pltpu.CompilerParams(
            collective_id=0, has_side_effects=True, vmem_limit_bytes=48 * 1024 * 1024
        ),
    )(a, b)


def body(
    features,
    bucket_ids,
    bucket_sizes,
    conv_weight,
    norm_gain,
    query_weight,
    key_weight,
    value_weight,
    out_weight,
    out_grad,
):
    rows_dev, cols_dev, width = features.shape[1:]
    count_y = lax.axis_size("sy")
    count_x = lax.axis_size("sx")
    count_d = lax.axis_size("dp")
    at_y, at_x = lax.axis_index("sy"), lax.axis_index("sx")
    rows, cols = rows_dev * count_y, cols_dev * count_x
    cells = rows * cols
    share = width // (count_y * count_x)
    first = (at_y * count_x + at_x) * share
    chosen = jnp.arange(bucket_sizes.shape[0], dtype=jnp.int32) == bucket_ids[0]
    height = jnp.sum(jnp.where(chosen, bucket_sizes[:, 0], 0))
    breadth = jnp.sum(jnp.where(chosen, bucket_sizes[:, 1], 0))
    valid = (jnp.arange(rows, dtype=jnp.int32)[:, None] < height) & (
        jnp.arange(cols, dtype=jnp.int32)[None, :] < breadth
    )
    valid_flat = valid.reshape(-1, 1).astype(F32)

    both = lax.all_gather(
        jnp.stack([features[0], out_grad[0]]), ("sy", "sx"), axis=0, tiled=False
    )
    both = both.reshape(count_y, count_x, 2, rows_dev, cols_dev, width)
    both = both.transpose(2, 0, 3, 1, 4, 5).reshape(2, rows, cols, width)
    both = jnp.where(valid[None, :, :, None], both, jnp.zeros((), BF16))
    xin = both[0]
    grad_b = both[1].reshape(cells, width)

    patches = patch_rows(jnp.pad(xin, ((1, 1), (1, 1), (0, 0))), rows, cols)
    pre = jnp.dot(patches, conv_weight, preferred_element_type=F32)
    hidden = (valid_flat * (xin.reshape(cells, width).astype(F32) + jax.nn.silu(pre))).astype(BF16)
    normed_f, pullback = jax.vjp(lambda value: layer_norm(value, norm_gain), hidden.astype(F32))
    normed = normed_f.astype(BF16)
    query = jnp.dot(normed, query_weight, preferred_element_type=F32).astype(BF16)
    keys = jnp.dot(normed, key_weight, preferred_element_type=F32).astype(BF16)
    values = jnp.dot(normed, value_weight, preferred_element_type=F32).astype(BF16)
    grad_context = dot_t(grad_b, out_weight, 1, 1).astype(BF16)
    context, dquery, dkey, dvalue = attention(
        valid_flat.reshape(1, cells), query, keys, values, grad_context, HEADS
    )

    def own_cells(array):
        grid = array.reshape(rows, cols, -1)
        tile = lax.dynamic_slice(
            grid,
            (at_y * rows_dev, at_x * cols_dev, 0),
            (rows_dev, cols_dev, grid.shape[2]),
        )
        return tile.reshape(rows_dev * cols_dev, -1)

    def own_columns(array):
        return lax.dynamic_slice_in_dim(array, first, share, axis=1)

    block = (
        own_cells(valid_flat)
        * (
            own_cells(hidden).astype(F32)
            + jnp.dot(own_cells(context), out_weight, preferred_element_type=F32)
        )
    ).astype(BF16)

    dthree = jnp.concatenate(
        [own_columns(dquery), own_columns(dkey), own_columns(dvalue)], axis=1
    )
    squares = jnp.concatenate(
        [dot_t(normed, dthree, 0, 0), dot_t(context, own_columns(grad_b), 0, 0)], axis=1
    ).astype(BF16)
    squares = squares.reshape(count_d, width // count_d, 4 * share)

    dnormed = (
        dot_t(dquery, query_weight, 1, 1)
        + dot_t(dkey, key_weight, 1, 1)
        + dot_t(dvalue, value_weight, 1, 1)
    )
    dhidden = grad_b.astype(F32) + pullback(dnormed)[0]
    sig = jax.nn.sigmoid(pre)
    dpre = (valid_flat * dhidden * sig * (1.0 + pre * (1.0 - sig))).astype(BF16)
    dpre_t = lax.dynamic_slice_in_dim(dpre.T, first, share, axis=0)
    piece = patches.shape[1] // count_d
    lanes = -(-piece // 128) * 128
    conv_t = jnp.dot(dpre_t, patches, preferred_element_type=F32).astype(BF16)
    conv_t = conv_t.reshape(share, count_d, piece).transpose(1, 0, 2)
    conv_t = jnp.pad(conv_t, ((0, 0), (0, 0), (0, lanes - piece)))

    conv_sum, square_sum = exchange(conv_t, squares)
    grad_cv = conv_sum[:, :piece].T
    grads = [square_sum[:, i * share : (i + 1) * share] for i in range(4)]
    return (block.reshape(1, rows_dev, cols_dev, width), grad_cv, *grads)


def solution(mesh):
    placed = (
        P("dp", "sy", "sx", None),
        P("dp"),
        P(),
        P(),
        P(),
        P(),
        P(),
        P(),
        P(),
        P("dp", "sy", "sx", None),
    )
    return jax.shard_map(
        body,
        mesh=mesh,
        in_specs=placed,
        out_specs=(
            P("dp", "sy", "sx", None),
            P("dp", ("sy", "sx")),
            P("dp", ("sy", "sx")),
            P("dp", ("sy", "sx")),
            P("dp", ("sy", "sx")),
            P("dp", ("sy", "sx")),
        ),
        check_vma=False,
    )
```

time: 754 us -> 160 us (0.21)
  waiting for transfers between devices: 552 us -> 16.4 us
  Pallas kernels: 0 us -> 76.6 us
  matrix products: 87.1 us -> 21.5 us
  blocking collectives: 44.1 us -> 0 us
  starting transfers between devices: 9.67 us -> 0.04 us
  local copies, waits for them, and re-layouts: 29.6 us -> 22 us
    reduce_scatter x5 -> x0, waiting for transfers between devices: 434 us -> none  [the longest x1 238 us: body(): lax.psum_scatter(grad_cv, 'dp', scatter_dimension=0, tiled=True)]
    unnamed x15 -> x1, waiting for transfers between devices: 116 us -> 0.02 us
    pallas_call x0 -> x2, Pallas kernels: none -> 76.6 us  [the longest x1 63.3 us: exchange(): pl.pallas_call(functools.partial(exchange_kernel, count), in_specs=[vmem,...]
    dot_general x84 -> x12, matrix products: 87.1 us -> 21.5 us  [the longest x6 8.52 us: dot_t(): lax.dot_general(a, b, (((ca,), (cb,)), ((), ())), preferred_element_type=...]
    all_gather x6 -> x0, blocking collectives: 44.1 us -> none  [the longest x1 8.46 us: body(): lax.all_gather(query, ('sy', 'sx'), axis=0, tiled=True)]
    unnamed x284 -> x32, local copies, waits for them, and re-layouts: 23.3 us -> 4.29 us
    all_gather x0 -> x1, waiting for transfers between devices: none -> 16.4 us  [body(): lax.all_gather(jnp.stack([features[0], out_grad[0]]), ('sy', 'sx'), axis=...]
    ppermute x4 -> x0, starting transfers between devices: 9.04 us -> none  [the longest x2 6.45 us: extended(): lax.ppermute(lax.slice_in_dim(block, block.shape[dim] - width, None, axis...]
  transfers between devices with their start and end apart: 14 -> 1, of which waited for: 11 -> 1; matrix products, arithmetic and copies ran while one was open for 10% -> 2% of each run, Pallas kernels for 0% -> 0%
where the time goes in v1:
time: 160 us; the launch traced here: 157 us
  Pallas kernels  76.6 us (48%)
  local copies, waits for them, and re-layouts  22 us (14%)
  matrix products  21.5 us (13%)
  waiting for transfers between devices  16.4 us (10%)
  between operations  15 us (9%)
  other arithmetic  5.93 us (4%)
    pallas_call x1, Pallas kernels, exchange(): pl.pallas_call(functools.partial(exchange_kernel, count), in_specs=[vmem,...  63.3 us
    all_gather x1, waiting for transfers between devices, body(): lax.all_gather(jnp.stack([features[0], out_grad[0]]), ('sy', 'sx'), axis=...  16.4 us
    pallas_call x1, Pallas kernels, attention(): pl.pallas_call(functools.partial(attention_kernel, width), grid=(heads //...  13.2 us
    dot_general x6, matrix products, dot_t(): lax.dot_general(a, b, (((ca,), (cb,)), ((), ())), preferred_element_type=...  8.52 us
    dot_general x1, matrix products, body(): pre = jnp.dot(patches, conv_weight, preferred_element_type=F32)  6.45 us
    reshape x2, local copies, waits for them, and re-layouts, body(): conv_t = conv_t.reshape(share, count_d, piece).transpose(1, 0, 2)  6.37 us
    unnamed x32, local copies, waits for them, and re-layouts  4.29 us
    another operation x2, local copies, waits for them, and re-layouts  3.98 us
  transfers between devices with their start and end apart: 1, of which 1 were waited for; matrix products, arithmetic and copies ran while one was open for 2% of the time, Pallas kernels for 0%

profile of v1, /device:TPU:24, one launch (start us, length us, event | category | flops | bytes accessed | tf_op | source)
XLA Modules:
  0.0 157.5 jit_solution(6763878091656359614)
XLA Ops:
  7.2 1.8 %pad_maximum_fusion.1 = bf16[2,8,16,640]{3,2,1,0:T(8,128)(2,1)} fusion(bf16[1,8,16,640]{3,2,1,0:T(8,128)(2,1)} %param.19, bf16[1,8,16,640]{3,2,1,0:T(8,128)(2,1)} %param.10), kind=kLoop, calls=%fused_computation.51 | loop fusion | flops 163840 | bytes 655360 | tf_op jit(solution)/shard_map/stack | solution.py:166
  9.7 1.4 fusion.31
  13.0 16.4 %all-gather.3.cloned.1.call-done = bf16[8,8,16,640]{3,2,1,0:T(8,128)(2,1)} async-done(((bf16[2,8,16,640]{3,2,1,0:T(8,128)(2,1)}), bf16[8,8,16,640]{3,2,1,0:T(8,128)(2,1)}) %all-gather.3.cloned.1.call-update) | async-done | bytes 1310736 | tf_op jit(solution)/shard_map/all_gather | solution.py:165
  29.4 1.4 copy.23
  33.4 1.4 slice-done.1
  34.8 6.4 %convert_reduce_fusion = (f32[512]{0:T(512)S(1)}, bf16[512,640]{1,0:T(8,128)(2,1)S(1)}, f32[512,640]{1,0:T(8,128)}, f32[512,640]{1,0:T(8,128)}) fusion(bf16[1,16,32,640]{3,2,1,0:T(8,128)(2,1)S(1)} %get-tuple-element.27, f32[512]{0:T(512)S(1)} %reshape.214, bf16[512,5760]{1,0:T(8,128)(2,1)S(1)} %constant_dynamic-update-slice_fusion, ...), kind=kOutput, calls=%fused_computation.4 | convolution fusion | flops 3778149888 | bytes 17207296 | tf_op jit(solution)/shard_map/dot_general | solution.py:175
  41.6 0.8 convolution_convert_fusion.4.q_ref
  42.8 0.8 convolution_convert_fusion.3.k_ref
  43.6 0.8 convolution_convert_fusion.2.v_ref
  45.5 13.2 %shard_map.145 = (bf16[512,640]{1,0:T(8,128)(2,1)S(1)}, bf16[512,640]{1,0:T(8,128)(2,1)S(1)}, bf16[512,640]{1,0:T(8,128)(2,1)S(1)}, bf16[512,640]{1,0:T(8,128)(2,1)S(1)}) custom-call(f32[1,512]{1,0:T(1,128)S(1)} %reshape.216.valid_ref, bf16[512,640]{1,0:T(8,128)(2,1)S(1)} %convolution_convert_fusion.4.q_ref, ...), custom_call_target="tpu_custom_call" | custom-call | flops 2013265920 | bytes 5242880 | tf_op jit(solution)/shard_map/pallas_call | solution.py:60
  59.6 0.9 constant_dynamic-slice_fusion.2
  61.2 1.0 constant_dynamic-slice_fusion
  62.2 0.9 fusion.8
  63.7 3.0 %convolution_convert_fusion = bf16[160,5760]{1,0:T(8,128)(2,1)S(1)} fusion(bf16[512,5760]{1,0:T(8,128)(2,1)S(1)} %constant_dynamic-update-slice_fusion, f32[512,640]{1,0:T(8,128)} %get-tuple-element.42, s32[]{:T(128)S(6)} %select_n.33, f32[512,640]{1,0:T(8,128)S(1)} %get-tuple-element.21, f32[512,640]{1,0:T(8,128)} %get-tuple-element.24, ...), kind=kOutput, calls=%fused_computation | convolution fusion | flops 945459200 | bytes 9580548 | tf_op jit(solution)/shard_map/dot_general | solution.py:226
  66.7 4.5 %reshape.213 = bf16[160,8,720]{2,1,0:T(8,128)(2,1)} reshape(bf16[160,5760]{1,0:T(8,128)(2,1)S(1)} %convolution_convert_fusion) | data formatting | bytes 3686400 | tf_op jit(solution)/shard_map/reshape | solution.py:227
  71.1 1.9 %copy.28 = bf16[160,8,720]{2,0,1:T(8,128)(2,1)S(1)} copy(bf16[160,8,720]{2,1,0:T(8,128)(2,1)} %reshape.213) | data formatting | bytes 3686400 | tf_op jit(solution)/shard_map/reshape | solution.py:227
  73.1 2.2 %convolution_convert_fusion.6 = bf16[640,160]{0,1:T(8,128)(2,1)} fusion(bf16[512,640]{1,0:T(8,128)(2,1)S(1)} %get-tuple-element.12, bf16[512,640]{1,0:T(8,128)(2,1)} %bitcast.72, s32[]{:T(128)S(6)} %select_n.33), kind=kOutput, calls=%fused_computation.26 | convolution fusion | flops 104960000 | bytes 1122308 | tf_op jit(solution)/shard_map/dot_general | solution.py:28
  75.2 1.8 %copy.26 = bf16[640,160]{1,0:T(8,128)(2,1)} copy(bf16[640,160]{0,1:T(8,128)(2,1)} %convolution_convert_fusion.6) | data formatting | bytes 409600 | tf_op jit(solution)/shard_map/convert.5
  77.1 3.1 %convolution_convert_fusion.5 = bf16[640,480]{0,1:T(8,128)(2,1)} fusion(bf16[512,160]{1,0:T(8,128)(2,1)} %get-tuple-element.45, bf16[512,160]{1,0:T(8,128)(2,1)} %get-tuple-element.46, bf16[512,160]{1,0:T(8,128)(2,1)} %constant_dynamic-slice_fusion.2, bf16[512,640]{1,0:T(8,128)(2,1)} %copy-done.1, f32[640]{0:T(1024)S(1)} %copy-done.9, f32[512]{0:T(512)S(1)} %fusion.30, ...), kind=kOutput, calls=%fused_computation.16 | convolution fusion | flops 317992960 | bytes 1767936 | tf_op jit(solution)/shard_map/dot_general | solution.py:28
  80.2 2.2 %copy.25 = bf16[640,480]{1,0:T(8,128)(2,1)} copy(bf16[640,480]{0,1:T(8,128)(2,1)} %convolution_convert_fusion.5) | data formatting | bytes 1228800 | tf_op jit(solution)/shard_map/convert.6
  82.6 0.9 copy-done.2
  83.7 63.3 %shard_map.146 = (f32[160,768]{1,0:T(8,128)S(1)}, f32[80,640]{1,0:T(8,128)S(1)}) custom-call(bf16[8,160,768]{2,1,0:T(8,128)(2,1)S(1)} %pad.9.a_ref, bf16[8,80,640]{2,1,0:T(8,128)(2,1)S(1)} %pad_maximum_fusion.b_ref), custom_call_target="tpu_custom_call" | custom-call | tf_op jit(solution)/shard_map/pallas_call | solution.py:116
  148.7 0.9 constant_dynamic-slice_fusion.3
  149.6 1.0 fusion.10
  (59 shorter events, 10.2 us)
Async XLA Ops:
  7.2 36.4 %copy-start = (bf16[640,640]{1,0:T(8,128)(2,1)S(1)}, bf16[640,640]{1,0:T(8,128)(2,1)}, u32[]{:S(2)}) copy-start(bf16[640,640]{1,0:T(8,128)(2,1)} %param.17) | copy-start | bytes 2457604
  7.2 22.2 %all-gather.3.cloned.1.call-start = ((), (), s32[]{:S(2)}) async-start(), calls=%async_computation | async-start | bytes 1638400 | tf_op jit(solution)/shard_map/all_gather | solution.py:165
  31.2 13.2 %copy-start.3 = (bf16[1,16,32,640]{3,2,1,0:T(8,128)(2,1)}, bf16[1,16,32,640]{3,2,1,0:T(8,128)(2,1)S(1)}, u32[]{:S(2)}) copy-start(bf16[1,16,32,640]{3,2,1,0:T(8,128)(2,1)S(1)} %get-tuple-element.25) | copy-start | bytes 1966084
  31.2 2.1 %slice-start = ((s8[7372800]{0:T(1024)(128)(4,1)}), s8[3178496]{0:T(1024)(128)(4,1)S(1)}, s32[]{:S(2)}) async-start(s8[7372800]{0:T(1024)(128)(4,1)} %bitcast.78), calls=%async_computation.1 | async-start | bytes 6356992
  32.0 2.7 %slice-start.1 = ((s8[7372800]{0:T(1024)(128)(4,1)}), s8[4194304]{0:T(1024)(128)(4,1)S(1)}, s32[]{:S(2)}) async-start(s8[7372800]{0:T(1024)(128)(4,1)} %bitcast.78), calls=%async_computation.2 | async-start | bytes 8388608
  34.8 6.8 %copy-start.5 = (bf16[640,640]{1,0:T(8,128)(2,1)S(1)}, bf16[640,640]{1,0:T(8,128)(2,1)}, u32[]{:S(2)}) copy-start(bf16[640,640]{1,0:T(8,128)(2,1)} %param.15) | copy-start | bytes 2457604
  34.8 6.8 %copy-start.9 = (f32[640]{0:T(1024)S(1)}, f32[640]{0:T(1024)}, u32[]{:S(2)}) copy-start(f32[640]{0:T(1024)} %param.14) | copy-start | bytes 7684
  41.2 21.9 %copy-start.1 = (bf16[512,640]{1,0:T(8,128)(2,1)}, bf16[512,640]{1,0:T(8,128)(2,1)S(1)}, u32[]{:S(2)}) copy-start(bf16[512,640]{1,0:T(8,128)(2,1)S(1)} %get-tuple-element.23) | copy-start | bytes 1966084
  41.6 1.1 copy-start.8
  43.6 1.1 copy-start.6
  82.4 1.1 copy-start.2
  82.4 1.2 copy-start.4
  147.0 2.6 %copy-start.7 = (bf16[640,640]{1,0:T(8,128)(2,1)S(1)}, bf16[640,640]{1,0:T(8,128)(2,1)}, u32[]{:S(2)}) copy-start(bf16[640,640]{1,0:T(8,128)(2,1)} %param.18) | copy-start | bytes 2457604
Sparse Core Ops, SparseCore 0:
  10.1 19.1 all-gather.2

commit v2 on v1

v2 whole, which is shorter than its diff:
```python
import functools

import jax
import jax.numpy as jnp
from jax import lax
from jax.experimental import pallas as pl
from jax.experimental.pallas import tpu as pltpu
from jax.sharding import PartitionSpec as P

HEADS = 10
F32 = jnp.float32
BF16 = jnp.bfloat16


VMEM_LIMIT = 56 * 1024 * 1024
MESH = pl.DeviceIdType.MESH


def dot_t(a, b, ca, cb):
    return lax.dot_general(a, b, (((ca,), (cb,)), ((), ())), preferred_element_type=F32)


def attention_kernel(width, valid_ref, q_ref, k_ref, v_ref, g_ref, c_ref, dq_ref, dk_ref, dv_ref):
    scale = width ** (-0.5)
    mask = valid_ref[...] > 0.0
    parts = ([], [], [], [])
    for start in range(0, q_ref.shape[1], width):
        q = q_ref[:, start : start + width]
        k = k_ref[:, start : start + width]
        v = v_ref[:, start : start + width]
        g = g_ref[:, start : start + width]
        scores = jnp.where(mask, dot_t(q, k, 1, 1) * scale, -1e30)
        expo = jnp.exp(scores - jnp.max(scores, axis=-1, keepdims=True))
        probs = expo * (1.0 / jnp.sum(expo, axis=-1, keepdims=True))
        probs_b = probs.astype(BF16)
        dprob = dot_t(g, v, 1, 1)
        delta = jnp.sum(probs * dprob, axis=-1, keepdims=True)
        dscore = (probs * (dprob - delta) * scale).astype(BF16)
        parts[0].append(dot_t(probs_b, v, 1, 0))
        parts[1].append(dot_t(dscore, k, 1, 0))
        parts[2].append(dot_t(dscore, q, 0, 0))
        parts[3].append(dot_t(probs_b, g, 0, 0))
    for ref, part in zip((c_ref, dq_ref, dk_ref, dv_ref), parts):
        ref[...] = jnp.concatenate(part, axis=-1).astype(BF16)


def attention(valid_row, query, keys, values, grads, heads):
    cells, channels = query.shape
    width = channels // heads
    block = pl.BlockSpec((cells, 2 * width), lambda i: (0, i))
    shape = jax.ShapeDtypeStruct((cells, channels), BF16)
    return pl.pallas_call(
        functools.partial(attention_kernel, width),
        grid=(heads // 2,),
        in_specs=[pl.BlockSpec((1, cells), lambda i: (0, 0))] + [block] * 4,
        out_specs=[block] * 4,
        out_shape=[shape] * 4,
        compiler_params=pltpu.CompilerParams(vmem_limit_bytes=48 * 1024 * 1024),
        cost_estimate=pl.CostEstimate(
            flops=12 * cells * cells * channels,
            bytes_accessed=16 * cells * channels,
            transcendentals=heads * cells * cells,
        ),
    )(valid_row, query, keys, values, grads)


def front_kernel(
    f_ref, g_ref, w_ref, valid_ref, gain_ref,
    s_ref, gb_ref, pre_ref, hid_ref, norm_ref,
    grid, weight, w_sem, own_sem, y_send, y_recv, x_send, x_recv,
):
    count_y, count_x = lax.axis_size("sy"), lax.axis_size("sx")
    at_y, at_x = lax.axis_index("sy"), lax.axis_index("sx")
    rows_dev, cols_dev, width = f_ref.shape
    rows, cols = grid.shape[1:3]
    cells = rows * cols
    barrier = pltpu.get_barrier_semaphore()
    for step in range(1, count_y):
        pl.semaphore_signal(
            barrier, inc=1, device_id={"sy": lax.rem(at_y + step, count_y)}, device_id_type=MESH
        )
    for step in range(1, count_x):
        pl.semaphore_signal(
            barrier, inc=1, device_id={"sx": lax.rem(at_x + step, count_x)}, device_id_type=MESH
        )
    pl.semaphore_wait(barrier, count_y + count_x - 2)

    def tile(which, y):
        return grid.at[
            which,
            pl.ds(y * rows_dev, rows_dev),
            pl.ds(pl.multiple_of(at_x * cols_dev, cols_dev), cols_dev),
        ]

    fetch = pltpu.make_async_copy(w_ref, weight, w_sem)
    locals_, ups, acrosses = [], [[], []], [[], []]
    for which, ref in enumerate((f_ref, g_ref)):
        for step in range(1, count_y):
            copy = pltpu.make_async_remote_copy(
                src_ref=ref,
                dst_ref=tile(which, at_y),
                send_sem=y_send.at[which, step - 1],
                recv_sem=y_recv.at[which, step - 1],
                device_id={"sy": lax.rem(at_y + step, count_y)},
                device_id_type=MESH,
            )
            copy.start()
            ups[which].append(copy)
        own = pltpu.make_async_copy(ref, tile(which, at_y), own_sem.at[which])
        own.start()
        locals_.append(own)
    fetch.start()

    def across(which, back):
        y = lax.rem(at_y - back + count_y, count_y)
        for step in range(1, count_x):
            copy = pltpu.make_async_remote_copy(
                src_ref=(f_ref, g_ref)[which] if back == 0 else tile(which, y),
                dst_ref=tile(which, y),
                send_sem=x_send.at[which, back, step - 1],
                recv_sem=x_recv.at[which, back, step - 1],
                device_id={"sx": lax.rem(at_x + step, count_x)},
                device_id_type=MESH,
            )
            copy.start()
            acrosses[which].append(copy)

    across(0, 0)
    across(1, 0)
    for back in range(1, count_y):
        ups[0][back - 1].wait_recv()
        across(0, back)
    locals_[0].wait()
    for copy in acrosses[0]:
        copy.wait_recv()

    edge = jnp.zeros((cols, width), BF16)
    for shift in range(3):
        s_ref[shift, 0:cols, :] = edge
        s_ref[shift, cells + cols : cells + 2 * cols, :] = edge

    def build(r, carry):
        at = pl.ds(pl.multiple_of(r * cols, cols), cols)
        to = pl.ds(pl.multiple_of((r + 1) * cols, cols), cols)
        line = grid[0, r].astype(F32) * valid_ref[at, :]
        zero = jnp.zeros((1, width), F32)
        s_ref[0, to, :] = jnp.concatenate([zero, line[:-1]], axis=0).astype(BF16)
        s_ref[1, to, :] = line.astype(BF16)
        s_ref[2, to, :] = jnp.concatenate([line[1:], zero], axis=0).astype(BF16)
        return carry

    lax.fori_loop(0, rows, build, 0)
    for back in range(1, count_y):
        ups[1][back - 1].wait_recv()
        across(1, back)
    fetch.wait()

    def tap(t, carry):
        dy, dx = t // 3, t % 3
        part = jnp.dot(
            s_ref[dx, pl.ds(pl.multiple_of(dy * cols, cols), cells), :],
            weight[pl.ds(pl.multiple_of(t * width, width), width), :],
            preferred_element_type=F32,
        )
        pre_ref[...] += part
        return carry

    pre_ref[...] = jnp.zeros_like(pre_ref)
    lax.fori_loop(0, 9, tap, 0)
    locals_[1].wait()
    for copy in acrosses[1]:
        copy.wait_recv()

    def finish(r, carry):
        at = pl.ds(pl.multiple_of(r * cols, cols), cols)
        valid = valid_ref[at, :]
        gb_ref[at, :] = (grid[1, r].astype(F32) * valid).astype(BF16)
        pre = pre_ref[at, :]
        xin = s_ref[1, pl.ds(pl.multiple_of((r + 1) * cols, cols), cols), :].astype(F32)
        hidden = (valid * (xin + pre * jax.nn.sigmoid(pre))).astype(BF16)
        hid_ref[at, :] = hidden
        hidden = hidden.astype(F32)
        centred = hidden - jnp.mean(hidden, axis=-1, keepdims=True)
        spread = jnp.mean(centred * centred, axis=-1, keepdims=True)
        norm_ref[at, :] = (centred * lax.rsqrt(spread + 1e-05) * gain_ref[...]).astype(BF16)
        return carry

    lax.fori_loop(0, rows, finish, 0)
    for group in ups + acrosses:
        for copy in group:
            copy.wait_send()


def front(features, out_grad, conv_weight, valid, gain):
    count_y, count_x = lax.axis_size("sy"), lax.axis_size("sx")
    rows_dev, cols_dev, width = features.shape
    rows, cols = rows_dev * count_y, cols_dev * count_x
    cells = rows * cols
    vmem = pl.BlockSpec(memory_space=pltpu.VMEM)
    anywhere = pl.BlockSpec(memory_space=pl.ANY)
    dma = pltpu.SemaphoreType.DMA
    return pl.pallas_call(
        front_kernel,
        in_specs=[anywhere, anywhere, anywhere, vmem, vmem],
        out_specs=[vmem] * 5,
        out_shape=[
            jax.ShapeDtypeStruct((3, cells + 2 * cols, width), BF16),
            jax.ShapeDtypeStruct((cells, width), BF16),
            jax.ShapeDtypeStruct((cells, width), F32),
            jax.ShapeDtypeStruct((cells, width), BF16),
            jax.ShapeDtypeStruct((cells, width), BF16),
        ],
        scratch_shapes=[
            pltpu.VMEM((2, rows, cols, width), BF16),
            pltpu.VMEM(conv_weight.shape, BF16),
            dma,
            dma((2,)),
            dma((2, count_y - 1)),
            dma((2, count_y - 1)),
            dma((2, count_y, count_x - 1)),
            dma((2, count_y, count_x - 1)),
        ],
        compiler_params=pltpu.CompilerParams(
            collective_id=1, has_side_effects=True, vmem_limit_bytes=VMEM_LIMIT
        ),
    )(features, out_grad, conv_weight, valid, gain)


def back_kernel(
    share, sq_ref, dq_ref, dk_ref, dv_ref, wq_ref, wk_ref, wv_ref, wo_ref,
    gb_ref, hid_ref, pre_ref, ctx_ref, valid_ref, gain_ref, s_ref,
    cv_out, sq_out, block_out,
    own, own_t, taps, cv, cv_pair, sq_pair, cv_sum, sq_sum, cv_got, sq_got,
    pair_send, pair_recv, far_send, far_recv,
):
    count = lax.axis_size("dp")
    half = count // 2
    me = lax.axis_index("dp")
    level, bit = me // 2, me % 2
    partner = me + 1 - 2 * bit
    at_y, at_x = lax.axis_index("sy"), lax.axis_index("sx")
    place = at_y * lax.axis_size("sx") + at_x
    cells, width = gb_ref.shape
    cols = s_ref.shape[1] - cells
    cols = cols // 2
    barrier = pltpu.get_barrier_semaphore()
    pl.semaphore_signal(barrier, inc=1, device_id={"dp": partner}, device_id_type=MESH)
    for step in range(1, half):
        pl.semaphore_signal(
            barrier,
            inc=1,
            device_id={"dp": 2 * lax.rem(level + step, half) + bit},
            device_id_type=MESH,
        )
    pl.semaphore_wait(barrier, half)

    order = list(range(1, half)) + [0]

    def to_partner(which, src, got):
        copies = {}
        for step in order:
            chunk = 2 * lax.rem(level + step, half) + 1 - bit
            copies[step] = pltpu.make_async_remote_copy(
                src_ref=src.at[chunk],
                dst_ref=got.at[step],
                send_sem=pair_send.at[which, step],
                recv_sem=pair_recv.at[which, step],
                device_id={"dp": partner},
                device_id_type=MESH,
            )
            copies[step].start()
        return copies

    def to_far(which, near, src, got, total, landed):
        copies = {}
        for step in order[:-1]:
            peer = 2 * lax.rem(level + step, half) + bit
            near[step].wait_recv()
            total[step - 1] = (src[peer].astype(F32) + got[step].astype(F32)).astype(BF16)
            copies[step] = pltpu.make_async_remote_copy(
                src_ref=total.at[step - 1],
                dst_ref=landed.at[step - 1],
                send_sem=far_send.at[which, step - 1],
                recv_sem=far_recv.at[which, step - 1],
                device_id={"dp": peer},
                device_id_type=MESH,
            )
            copies[step].start()
        return copies

    def collect(near, far, src, got, landed, out):
        near[0].wait_recv()
        value = src[me].astype(F32) + got[0].astype(F32)
        for step in order[:-1]:
            far[step].wait_recv()
            value += landed[step - 1].astype(F32)
        out[...] = value

    sq_near = to_partner(0, sq_ref, sq_pair)

    rows_at = cells // 4

    def backward(r, carry):
        at = pl.ds(pl.multiple_of(r * rows_at, rows_at), rows_at)
        dnormed = dot_t(dq_ref[at, :], wq_ref[...], 1, 1)
        dnormed += dot_t(dk_ref[at, :], wk_ref[...], 1, 1)
        dnormed += dot_t(dv_ref[at, :], wv_ref[...], 1, 1)
        hidden = hid_ref[at, :].astype(F32)
        centred = hidden - jnp.mean(hidden, axis=-1, keepdims=True)
        spread = jnp.mean(centred * centred, axis=-1, keepdims=True)
        rstd = lax.rsqrt(spread + 1e-05)
        unit = centred * rstd
        up = dnormed * gain_ref[...]
        down = up - jnp.mean(up, axis=-1, keepdims=True)
        down = rstd * (down - unit * jnp.mean(up * unit, axis=-1, keepdims=True))
        pre = pre_ref[at, :]
        sig = jax.nn.sigmoid(pre)
        dpre = (gb_ref[at, :].astype(F32) + down) * sig * (1.0 + pre * (1.0 - sig))
        dpre = dpre * valid_ref[at, :]
        mine = dpre[:, 0:share]
        for index in range(1, width // share):
            mine = jnp.where(place == index, dpre[:, index * share : (index + 1) * share], mine)
        own[at, :] = mine
        return carry

    lax.fori_loop(0, 4, backward, 0)
    sq_far = to_far(0, sq_near, sq_ref, sq_pair, sq_sum, sq_got)
    own_t[...] = own[...].T.astype(BF16)
    for t in range(9):
        dy, dx = t // 3, t % 3
        taps[:, t * width : (t + 1) * width] = jnp.dot(
            own_t[...],
            s_ref[dx, dy * cols : dy * cols + cells, :],
            preferred_element_type=F32,
        )
    piece = taps.shape[1] // count
    spare = jnp.zeros((share, cv.shape[2] - piece), F32)
    for index in range(count):
        part = taps[:, index * piece : (index + 1) * piece]
        cv[index] = jnp.concatenate([part, spare], axis=1).astype(BF16)
    cv_near = to_partner(1, cv, cv_pair)

    rows_dev, cols_dev = block_out.shape[:2]
    rows_own = pl.ds(at_y * rows_dev, rows_dev)
    cols_own = pl.ds(pl.multiple_of(at_x * cols_dev, cols_dev), cols_dev)
    context = ctx_ref[rows_own, cols_own, :].reshape(rows_dev * cols_dev, width)
    made = jnp.dot(context, wo_ref[...], preferred_element_type=F32)
    for r in range(rows_dev):
        start = pl.multiple_of((at_y * rows_dev + r) * cols + at_x * cols_dev, cols_dev)
        line = pl.ds(start, cols_dev)
        value = hid_ref[line, :].astype(F32) + made[r * cols_dev : (r + 1) * cols_dev]
        block_out[r] = (value * valid_ref[line, :]).astype(BF16)

    cv_far = to_far(1, cv_near, cv, cv_pair, cv_sum, cv_got)
    collect(sq_near, sq_far, sq_ref, sq_pair, sq_got, sq_out)
    collect(cv_near, cv_far, cv, cv_pair, cv_got, cv_out)
    for group in (sq_near, sq_far, cv_near, cv_far):
        for copy in group.values():
            copy.wait_send()


def back(share, tile_shape, squares, arrays, context_grid, valid, gain, stack, piece):
    count = squares.shape[0]
    half = count // 2
    cells, width = arrays[0].shape
    lanes = -(-piece // 128) * 128
    vmem = pl.BlockSpec(memory_space=pltpu.VMEM)
    dma = pltpu.SemaphoreType.DMA
    conv_shape, square_shape = (share, lanes), squares.shape[1:]
    return pl.pallas_call(
        functools.partial(back_kernel, share),
        in_specs=[vmem] * 15,
        out_specs=[vmem] * 3,
        out_shape=[
            jax.ShapeDtypeStruct(conv_shape, F32),
            jax.ShapeDtypeStruct(square_shape, F32),
            jax.ShapeDtypeStruct(tile_shape, BF16),
        ],
        scratch_shapes=[
            pltpu.VMEM((cells, share), F32),
            pltpu.VMEM((share, cells), BF16),
            pltpu.VMEM((share, 9 * width), F32),
            pltpu.VMEM((count,) + conv_shape, BF16),
            pltpu.VMEM((half,) + conv_shape, BF16),
            pltpu.VMEM((half,) + square_shape, BF16),
            pltpu.VMEM((half - 1,) + conv_shape, BF16),
            pltpu.VMEM((half - 1,) + square_shape, BF16),
            pltpu.VMEM((half - 1,) + conv_shape, BF16),
            pltpu.VMEM((half - 1,) + square_shape, BF16),
            dma((2, half)),
            dma((2, half)),
            dma((2, half - 1)),
            dma((2, half - 1)),
        ],
        compiler_params=pltpu.CompilerParams(
            collective_id=2, has_side_effects=True, vmem_limit_bytes=VMEM_LIMIT
        ),
    )(squares, *arrays, context_grid, valid, gain, stack)


def body(
    features,
    bucket_ids,
    bucket_sizes,
    conv_weight,
    norm_gain,
    query_weight,
    key_weight,
    value_weight,
    out_weight,
    out_grad,
):
    rows_dev, cols_dev, width = features.shape[1:]
    count_y = lax.axis_size("sy")
    count_x = lax.axis_size("sx")
    count_d = lax.axis_size("dp")
    at_y, at_x = lax.axis_index("sy"), lax.axis_index("sx")
    rows, cols = rows_dev * count_y, cols_dev * count_x
    cells = rows * cols
    share = width // (count_y * count_x)
    first = (at_y * count_x + at_x) * share
    chosen = jnp.arange(bucket_sizes.shape[0], dtype=jnp.int32) == bucket_ids[0]
    height = jnp.sum(jnp.where(chosen, bucket_sizes[:, 0], 0))
    breadth = jnp.sum(jnp.where(chosen, bucket_sizes[:, 1], 0))
    valid = (jnp.arange(rows, dtype=jnp.int32)[:, None] < height) & (
        jnp.arange(cols, dtype=jnp.int32)[None, :] < breadth
    )
    valid_flat = valid.reshape(-1, 1).astype(F32)
    gain = norm_gain.reshape(1, width)

    stack, grad_b, pre, hidden, normed = front(
        features[0], out_grad[0], conv_weight, valid_flat, gain
    )
    query = jnp.dot(normed, query_weight, preferred_element_type=F32).astype(BF16)
    keys = jnp.dot(normed, key_weight, preferred_element_type=F32).astype(BF16)
    values = jnp.dot(normed, value_weight, preferred_element_type=F32).astype(BF16)
    grad_context = dot_t(grad_b, out_weight, 1, 1).astype(BF16)
    context, dquery, dkey, dvalue = attention(
        valid_flat.reshape(1, cells), query, keys, values, grad_context, HEADS
    )

    def own_columns(array):
        return lax.dynamic_slice_in_dim(array, first, share, axis=1)

    dthree = jnp.concatenate(
        [own_columns(dquery), own_columns(dkey), own_columns(dvalue)], axis=1
    )
    squares = jnp.concatenate(
        [dot_t(normed, dthree, 0, 0), dot_t(context, own_columns(grad_b), 0, 0)], axis=1
    ).astype(BF16)
    squares = squares.reshape(count_d, width // count_d, 4 * share)
    piece = conv_weight.shape[0] // count_d
    conv_sum, square_sum, block = back(
        share,
        features.shape[1:],
        squares,
        (dquery, dkey, dvalue, query_weight, key_weight, value_weight, out_weight,
         grad_b, hidden, pre),
        context.reshape(rows, cols, width),
        valid_flat,
        gain,
        stack,
        piece,
    )
    grad_cv = conv_sum[:, :piece].T
    grads = [square_sum[:, i * share : (i + 1) * share] for i in range(4)]
    return (block[None], grad_cv, *grads)


def solution(mesh):
    placed = (
        P("dp", "sy", "sx", None),
        P("dp"),
        P(),
        P(),
        P(),
        P(),
        P(),
        P(),
        P(),
        P("dp", "sy", "sx", None),
    )
    return jax.shard_map(
        body,
        mesh=mesh,
        in_specs=placed,
        out_specs=(
            P("dp", "sy", "sx", None),
            P("dp", ("sy", "sx")),
            P("dp", ("sy", "sx")),
            P("dp", ("sy", "sx")),
            P("dp", ("sy", "sx")),
            P("dp", ("sy", "sx")),
        ),
        check_vma=False,
    )
```

time: 160 us -> 115 us (0.72)
  waiting for transfers between devices: 16.4 us -> 0 us
  between operations: 15 us -> 1.48 us
  matrix products: 21.5 us -> 9.96 us
  local copies, waits for them, and re-layouts: 22 us -> 13.1 us
  Pallas kernels: 76.6 us -> 84.8 us
  other arithmetic: 5.93 us -> 3.89 us
    all_gather x1 -> x0, waiting for transfers between devices: 16.4 us -> none  [body(): lax.all_gather(jnp.stack([features[0], out_grad[0]]), ('sy', 'sx'), axis=...]
    dot_general x3 -> x0, matrix products: 10.4 us -> none  [the longest x1 6.45 us: body(): pre = jnp.dot(patches, conv_weight, preferred_element_type=F32)]
    pallas_call x1 -> x2, Pallas kernels: 63.3 us -> 71.8 us  [the longest x1 47.1 us: back(): pl.pallas_call(functools.partial(back_kernel, share), in_specs=[vmem] * 1...]
    reshape x2 -> x1, local copies, waits for them, and re-layouts: 6.37 us -> 1.27 us  [body(): gain = norm_gain.reshape(1, width)]
    dot_general x6 -> x3, matrix products: 8.52 us -> 4.83 us  [dot_t(): lax.dot_general(a, b, (((ca,), (cb,)), ((), ())), preferred_element_type=...]
    another operation x2, local copies, waits for them, and re-layouts: 3.98 us -> 1.49 us
    another operation x1 -> x0, other arithmetic: 1.82 us -> none  [body(): jnp.stack([features[0], out_grad[0]])]
    unnamed x32 -> x31, local copies, waits for them, and re-layouts: 4.29 us -> 5.13 us
  transfers between devices with their start and end apart: 1 -> 0, of which waited for: 1 -> 0; matrix products, arithmetic and copies ran while one was open for 2% -> 0% of each run, Pallas kernels for 0% -> 0%
where the time goes in v2:
time: 115 us; the launch traced here: 113 us
  Pallas kernels  84.8 us (74%)
  local copies, waits for them, and re-layouts  13.1 us (11%)
  matrix products  9.96 us (9%)
  other arithmetic  3.89 us (3%)
  between operations  1.48 us (1%)
    pallas_call x1, Pallas kernels, back(): pl.pallas_call(functools.partial(back_kernel, share), in_specs=[vmem] * 1...  47.1 us
    pallas_call x1, Pallas kernels, front(): pl.pallas_call(front_kernel, in_specs=[anywhere, anywhere, anywhere, vmem...  24.7 us
    pallas_call x1, Pallas kernels, attention(): pl.pallas_call(functools.partial(attention_kernel, width), grid=(heads //...  13 us
    unnamed x31, local copies, waits for them, and re-layouts  5.13 us
    dot_general x3, matrix products, dot_t(): lax.dot_general(a, b, (((ca,), (cb,)), ((), ())), preferred_element_type=...  4.83 us

profile of v2, /device:TPU:24, one launch (start us, length us, event | category | flops | bytes accessed | tf_op | source)
XLA Modules:
  0.0 113.2 jit_solution(2901091896311599995)
XLA Ops:
  1.3 1.4 %fusion.7 = (s32[]{:T(128)}, s32[]{:T(128)}) fusion(s32[8,2]{0,1:T(2,128)} %param.12, s32[]{:T(128)} %bitcast.23), kind=kLoop, calls=%fused_computation.21 | loop fusion | flops 38 | bytes 76 | tf_op jit(solution)/shard_map/reduce_sum | solution.py:423
  2.7 0.6 iota_compare_fusion
  3.3 0.7 iota_compare_fusion.1
  4.1 1.0 reshape.89.valid_ref
  5.0 1.3 %reshape.85.gain_ref = f32[1,640]{1,0:T(1,128)} reshape(f32[640]{0:T(1024)} %param.14) | data formatting | bytes 5120 | tf_op jit(solution)/shard_map/reshape | solution.py:429
  6.3 24.7 %shard_map.145 = (bf16[3,576,640]{2,1,0:T(8,128)(2,1)}, bf16[512,640]{1,0:T(8,128)(2,1)}, f32[512,640]{1,0:T(8,128)}, bf16[512,640]{1,0:T(8,128)(2,1)}, bf16[512,640]{1,0:T(8,128)(2,1)}) custom-call(bf16[8,16,640]{2,1,0:T(8,128)(2,1)} %bitcast.28, bf16[8,16,640]{2,1,0:T(8,128)(2,1)} %bitcast.29, bf16[5760,640]{1,0:T(8,128)(2,1)} %w_ref.1, ...), custom_call_target="tpu_custom_call" | custom-call | tf_op jit(solution)/shard_map/pallas_call | solution.py:202
  31.1 1.9 %convolution_convert_fusion.1.v_ref = bf16[512,640]{1,0:T(8,128)(2,1)S(1)} fusion(bf16[512,640]{1,0:T(8,128)(2,1)} %get-tuple-element.18, bf16[640,640]{1,0:T(8,128)(2,1)S(1)} %copy-done.10), kind=kOutput, calls=%fused_computation.1 | convolution fusion | flops 419758080 | bytes 2129920 | tf_op jit(solution)/shard_map/dot_general | solution.py:436
  33.0 1.6 %convolution_convert_fusion.2.k_ref = bf16[512,640]{1,0:T(8,128)(2,1)} fusion(bf16[512,640]{1,0:T(8,128)(2,1)S(1)} %copy-done.13, bf16[640,640]{1,0:T(8,128)(2,1)S(1)} %copy-done.9), kind=kOutput, calls=%fused_computation.2 | convolution fusion | flops 419758080 | bytes 2129920 | tf_op jit(solution)/shard_map/dot_general | solution.py:435
  34.6 1.6 %convolution_convert_fusion.3.q_ref = bf16[512,640]{1,0:T(8,128)(2,1)} fusion(bf16[512,640]{1,0:T(8,128)(2,1)S(1)} %copy-done.13, bf16[640,640]{1,0:T(8,128)(2,1)S(1)} %copy-done.8), kind=kOutput, calls=%fused_computation.3 | convolution fusion | flops 419758080 | bytes 2129920 | tf_op jit(solution)/shard_map/dot_general | solution.py:434
  36.2 1.6 %convolution_convert_fusion.g_ref = bf16[512,640]{1,0:T(8,128)(2,1)} fusion(bf16[512,640]{1,0:T(8,128)(2,1)S(1)} %copy-done.7, bf16[640,640]{1,0:T(8,128)(2,1)S(1)} %copy-done.11), kind=kOutput, calls=%fused_computation | convolution fusion | flops 419758080 | bytes 2129920 | tf_op jit(solution)/shard_map/dot_general | solution.py:20
  37.9 1.1 copy-done.4
  39.0 1.1 copy-done.5
  40.1 1.1 copy-done.6
  41.2 13.0 %shard_map.146 = (bf16[512,640]{1,0:T(8,128)(2,1)S(1)}, bf16[512,640]{1,0:T(8,128)(2,1)S(1)}, bf16[512,640]{1,0:T(8,128)(2,1)S(1)}, bf16[512,640]{1,0:T(8,128)(2,1)S(1)}) custom-call(f32[1,512]{1,0:T(1,128)S(1)} %reshape.88.valid_ref, bf16[512,640]{1,0:T(8,128)(2,1)S(1)} %copy-done.5, bf16[512,640]{1,0:T(8,128)(2,1)S(1)} %copy-done.4, ...), custom_call_target="tpu_custom_call" | custom-call | flops 2013265920 | bytes 5242880 | tf_op jit(solution)/shard_map/pallas_call | solution.py:52
  54.3 0.2 constant_dynamic-slice_fusion
  54.7 1.2 %copy-done.14 = bf16[512,640]{1,0:T(8,128)(2,1)S(1)} copy-done((bf16[512,640]{1,0:T(8,128)(2,1)S(1)}, bf16[512,640]{1,0:T(8,128)(2,1)}, u32[]{:S(2)}) %copy-start.14) | copy-done | bytes 655384
  55.8 1.7 %convolution_convert_fusion.4 = bf16[640,480]{0,1:T(8,128)(2,1)} fusion(bf16[512,640]{1,0:T(8,128)(2,1)S(1)} %copy-done.14, bf16[512,160]{1,0:T(8,128)(2,1)S(1)} %get-tuple-element.36, bf16[512,160]{1,0:T(8,128)(2,1)S(1)} %get-tuple-element.37, bf16[512,160]{1,0:T(8,128)(2,1)S(1)} %constant_dynamic-slice_fusion.2), kind=kOutput, calls=%fused_computation.4 | convolution fusion | flops 316354560 | bytes 1761280 | tf_op jit(solution)/shard_map/dot_general | solution.py:20
  57.6 1.3 %copy.19 = bf16[640,480]{1,0:T(8,128)(2,1)S(1)} copy(bf16[640,480]{0,1:T(8,128)(2,1)} %convolution_convert_fusion.4) | data formatting | bytes 1228800 | tf_op jit(solution)/shard_map/convert.5
  58.9 1.5 %convolution_convert_fusion.5 = bf16[640,160]{0,1:T(8,128)(2,1)S(1)} fusion(bf16[512,640]{1,0:T(8,128)(2,1)S(1)} %get-tuple-element.23, bf16[512,640]{1,0:T(8,128)(2,1)} %get-tuple-element.19.gb_ref, s32[]{:T(128)S(6)} %select_n.15), kind=kOutput, calls=%fused_computation.5 | convolution fusion | flops 104960000 | bytes 1122308 | tf_op jit(solution)/shard_map/dot_general | solution.py:20
  60.6 1.1 pad_maximum_fusion.sq_ref
  61.7 47.1 %shard_map.147 = (f32[160,768]{1,0:T(8,128)}, f32[80,640]{1,0:T(8,128)}, bf16[8,16,640]{2,1,0:T(8,128)(2,1)}) custom-call(bf16[8,80,640]{2,1,0:T(8,128)(2,1)} %pad_maximum_fusion.sq_ref, bf16[512,640]{1,0:T(8,128)(2,1)} %copy-done.1, bf16[512,640]{1,0:T(8,128)(2,1)} %copy-done.2, bf16[512,640]{1,0:T(8,128)(2,1)} %copy-done.3, bf16[640,640]{1,0:T(8,128)(2,1)} %wq_ref.1, ...), custom_call_target="tpu_custom_call" | custom-call | tf_op jit(solution)/shard_map/pallas_call | solution.py:370
  108.8 1.9 %slice_bitcast_fusion = f32[720,160]{0,1:T(8,128)} fusion(f32[160,768]{1,0:T(8,128)} %get-tuple-element.28), kind=kLoop, calls=%fused_computation.12 | loop fusion | bytes 921600 | tf_op jit(solution)/shard_map/transpose | solution.py:465
  110.7 1.9 %fusion.10 = (f32[80,160]{1,0:T(8,128)}, f32[80,160]{1,0:T(8,128)}, f32[80,160]{1,0:T(8,128)}, f32[80,160]{1,0:T(8,128)}) fusion(f32[80,640]{1,0:T(8,128)} %get-tuple-element.29), kind=kLoop, calls=%fused_computation.26 | loop fusion | bytes 409600 | tf_op jit(solution)/shard_map/slice | solution.py:466
  112.6 0.7 copy.24
  (30 shorter events, 0.5 us)
Async XLA Ops:
  6.3 24.7 %copy-start.10 = (bf16[640,640]{1,0:T(8,128)(2,1)S(1)}, bf16[640,640]{1,0:T(8,128)(2,1)}, u32[]{:S(2)}) copy-start(bf16[640,640]{1,0:T(8,128)(2,1)} %wv_ref.1) | copy-start | bytes 2457604
  31.0 2.0 %copy-start.9 = (bf16[640,640]{1,0:T(8,128)(2,1)S(1)}, bf16[640,640]{1,0:T(8,128)(2,1)}, u32[]{:S(2)}) copy-start(bf16[640,640]{1,0:T(8,128)(2,1)} %wk_ref.1) | copy-start | bytes 2457604
  31.0 2.0 %copy-start.13 = (bf16[512,640]{1,0:T(8,128)(2,1)S(1)}, bf16[512,640]{1,0:T(8,128)(2,1)}, u32[]{:S(2)}) copy-start(bf16[512,640]{1,0:T(8,128)(2,1)} %get-tuple-element.18) | copy-start | bytes 1966084
  33.0 1.6 %copy-start.8 = (bf16[640,640]{1,0:T(8,128)(2,1)S(1)}, bf16[640,640]{1,0:T(8,128)(2,1)}, u32[]{:S(2)}) copy-start(bf16[640,640]{1,0:T(8,128)(2,1)} %wq_ref.1) | copy-start | bytes 2457604
  34.6 1.6 %copy-start.7 = (bf16[512,640]{1,0:T(8,128)(2,1)S(1)}, bf16[512,640]{1,0:T(8,128)(2,1)}, u32[]{:S(2)}) copy-start(bf16[512,640]{1,0:T(8,128)(2,1)} %get-tuple-element.19.gb_ref) | copy-start | bytes 1966084
  34.6 1.6 %copy-start.11 = (bf16[640,640]{1,0:T(8,128)(2,1)S(1)}, bf16[640,640]{1,0:T(8,128)(2,1)}, u32[]{:S(2)}) copy-start(bf16[640,640]{1,0:T(8,128)(2,1)} %wo_ref.1) | copy-start | bytes 2457604
  37.9 1.1 copy-start.4
  39.0 1.1 copy-start.5
  40.1 1.1 copy-start.6
  54.2 3.3 %copy-start.1 = (bf16[512,640]{1,0:T(8,128)(2,1)}, bf16[512,640]{1,0:T(8,128)(2,1)S(1)}, u32[]{:S(2)}) copy-start(bf16[512,640]{1,0:T(8,128)(2,1)S(1)} %get-tuple-element.20.dq_ref) | copy-start | bytes 1966084
  54.2 3.3 %copy-start.2 = (bf16[512,640]{1,0:T(8,128)(2,1)}, bf16[512,640]{1,0:T(8,128)(2,1)S(1)}, u32[]{:S(2)}) copy-start(bf16[512,640]{1,0:T(8,128)(2,1)S(1)} %get-tuple-element.21.dk_ref) | copy-start | bytes 1966084
  54.3 3.3 %copy-start.3 = (bf16[512,640]{1,0:T(8,128)(2,1)}, bf16[512,640]{1,0:T(8,128)(2,1)S(1)}, u32[]{:S(2)}) copy-start(bf16[512,640]{1,0:T(8,128)(2,1)S(1)} %get-tuple-element.22.dv_ref) | copy-start | bytes 1966084
  54.3 4.6 %copy-start = (bf16[512,640]{1,0:T(8,128)(2,1)}, bf16[512,640]{1,0:T(8,128)(2,1)S(1)}, u32[]{:S(2)}) copy-start(bf16[512,640]{1,0:T(8,128)(2,1)S(1)} %get-tuple-element.23) | copy-start | bytes 1966084
  54.3 1.6 %copy-start.14 = (bf16[512,640]{1,0:T(8,128)(2,1)S(1)}, bf16[512,640]{1,0:T(8,128)(2,1)}, u32[]{:S(2)}) copy-start(bf16[512,640]{1,0:T(8,128)(2,1)} %get-tuple-element.18) | copy-start | bytes 1966084
  108.8 3.7 %copy-start.12 = (bf16[8,16,640]{2,1,0:T(8,128)(2,1)S(1)}, bf16[8,16,640]{2,1,0:T(8,128)(2,1)}, u32[]{:S(2)}) copy-start(bf16[8,16,640]{2,1,0:T(8,128)(2,1)} %get-tuple-element.27) | copy-start | bytes 491524

commit v3 on v2

--- a/solution.py
+++ b/solution.py
@@ -20,15 +20,33 @@
     return lax.dot_general(a, b, (((ca,), (cb,)), ((), ())), preferred_element_type=F32)
 
 
-def attention_kernel(width, valid_ref, q_ref, k_ref, v_ref, g_ref, c_ref, dq_ref, dk_ref, dv_ref):
+def bucket_size(ids_ref, sizes_ref):
+    height, breadth = jnp.int32(0), jnp.int32(0)
+    for index in range(sizes_ref.shape[0]):
+        height = jnp.where(ids_ref[0] == index, sizes_ref[index, 0], height)
+        breadth = jnp.where(ids_ref[0] == index, sizes_ref[index, 1], breadth)
+    return height, breadth
+
+
+def attention_kernel(
+    width, cols, ids_ref, sizes_ref, n_ref, gb_ref, wq_ref, wk_ref, wv_ref, wo_ref,
+    c_ref, dq_ref, dk_ref, dv_ref,
+):
     scale = width ** (-0.5)
-    mask = valid_ref[...] > 0.0
+    height, breadth = bucket_size(ids_ref, sizes_ref)
+    index = lax.broadcasted_iota(jnp.int32, (1, n_ref.shape[0]), 1)
+    mask = (index // cols < height) & (index % cols < breadth)
+    normed = n_ref[...]
+    q_both = jnp.dot(normed, wq_ref[...], preferred_element_type=F32).astype(BF16)
+    k_both = jnp.dot(normed, wk_ref[...], preferred_element_type=F32).astype(BF16)
+    v_both = jnp.dot(normed, wv_ref[...], preferred_element_type=F32).astype(BF16)
+    g_both = dot_t(gb_ref[...], wo_ref[...], 1, 1).astype(BF16)
     parts = ([], [], [], [])
-    for start in range(0, q_ref.shape[1], width):
-        q = q_ref[:, start : start + width]
-        k = k_ref[:, start : start + width]
-        v = v_ref[:, start : start + width]
-        g = g_ref[:, start : start + width]
+    for start in range(0, q_both.shape[1], width):
+        q = q_both[:, start : start + width]
+        k = k_both[:, start : start + width]
+        v = v_both[:, start : start + width]
+        g = g_both[:, start : start + width]
         scores = jnp.where(mask, dot_t(q, k, 1, 1) * scale, -1e30)
         expo = jnp.exp(scores - jnp.max(scores, axis=-1, keepdims=True))
         probs = expo * (1.0 / jnp.sum(expo, axis=-1, keepdims=True))
@@ -44,29 +62,33 @@
         ref[...] = jnp.concatenate(part, axis=-1).astype(BF16)
 
 
-def attention(valid_row, query, keys, values, grads, heads):
-    cells, channels = query.shape
+def attention(ids, sizes, normed, grad_b, weights, heads, cols):
+    cells, channels = normed.shape
     width = channels // heads
+    smem = pl.BlockSpec(memory_space=pltpu.SMEM)
+    whole = pl.BlockSpec((cells, channels), lambda i: (0, 0))
+    column = pl.BlockSpec((channels, 2 * width), lambda i: (0, i))
     block = pl.BlockSpec((cells, 2 * width), lambda i: (0, i))
     shape = jax.ShapeDtypeStruct((cells, channels), BF16)
     return pl.pallas_call(
-        functools.partial(attention_kernel, width),
+        functools.partial(attention_kernel, width, cols),
         grid=(heads // 2,),
-        in_specs=[pl.BlockSpec((1, cells), lambda i: (0, 0))] + [block] * 4,
+        in_specs=[smem, smem, whole, whole, column, column, column]
+        + [pl.BlockSpec((2 * width, channels), lambda i: (i, 0))],
         out_specs=[block] * 4,
         out_shape=[shape] * 4,
         compiler_params=pltpu.CompilerParams(vmem_limit_bytes=48 * 1024 * 1024),
         cost_estimate=pl.CostEstimate(
-            flops=12 * cells * cells * channels,
+            flops=12 * cells * cells * channels + 8 * cells * channels * channels,
             bytes_accessed=16 * cells * channels,
             transcendentals=heads * cells * cells,
         ),
-    )(valid_row, query, keys, values, grads)
+    )(ids, sizes, normed, grad_b, *weights)
 
 
 def front_kernel(
-    f_ref, g_ref, w_ref, valid_ref, gain_ref,
-    s_ref, gb_ref, pre_ref, hid_ref, norm_ref,
+    f_ref, g_ref, w_ref, ids_ref, sizes_ref, gain_ref,
+    s_ref, gb_ref, pre_ref, hid_ref, norm_ref, valid_ref,
     grid, weight, w_sem, own_sem, y_send, y_recv, x_send, x_recv,
 ):
     count_y, count_x = lax.axis_size("sy"), lax.axis_size("sx")
@@ -134,6 +156,7 @@
     for copy in acrosses[0]:
         copy.wait_recv()
 
+    height, breadth = bucket_size(ids_ref, sizes_ref)
     edge = jnp.zeros((cols, width), BF16)
     for shift in range(3):
         s_ref[shift, 0:cols, :] = edge
@@ -142,7 +165,10 @@
     def build(r, carry):
         at = pl.ds(pl.multiple_of(r * cols, cols), cols)
         to = pl.ds(pl.multiple_of((r + 1) * cols, cols), cols)
-        line = grid[0, r].astype(F32) * valid_ref[at, :]
+        column = lax.broadcasted_iota(jnp.int32, (cols, 1), 0)
+        valid = (column < jnp.where(r < height, breadth, 0)).astype(F32)
+        valid_ref[at, :] = valid
+        line = grid[0, r].astype(F32) * valid
         zero = jnp.zeros((1, width), F32)
         s_ref[0, to, :] = jnp.concatenate([zero, line[:-1]], axis=0).astype(BF16)
         s_ref[1, to, :] = line.astype(BF16)
@@ -155,60 +181,68 @@
         across(1, back)
     fetch.wait()
 
-    def tap(t, carry):
-        dy, dx = t // 3, t % 3
-        part = jnp.dot(
-            s_ref[dx, pl.ds(pl.multiple_of(dy * cols, cols), cells), :],
-            weight[pl.ds(pl.multiple_of(t * width, width), width), :],
-            preferred_element_type=F32,
-        )
-        pre_ref[...] += part
+    block = cells // 2
+
+    def convolve(r, carry):
+        total = None
+        for t in range(9):
+            dy, dx = t // 3, t % 3
+            part = jnp.dot(
+                s_ref[dx, pl.ds(pl.multiple_of(r * block + dy * cols, cols), block), :],
+                weight[t * width : (t + 1) * width, :],
+                preferred_element_type=F32,
+            )
+            total = part if total is None else total + part
+        pre_ref[pl.ds(pl.multiple_of(r * block, block), block), :] = total
         return carry
 
-    pre_ref[...] = jnp.zeros_like(pre_ref)
-    lax.fori_loop(0, 9, tap, 0)
+    lax.fori_loop(0, 2, convolve, 0)
     locals_[1].wait()
     for copy in acrosses[1]:
         copy.wait_recv()
 
+    gain = gain_ref[...].reshape(1, width)
+
     def finish(r, carry):
-        at = pl.ds(pl.multiple_of(r * cols, cols), cols)
+        at = pl.ds(pl.multiple_of(r * 2 * cols, cols), 2 * cols)
         valid = valid_ref[at, :]
-        gb_ref[at, :] = (grid[1, r].astype(F32) * valid).astype(BF16)
+        gb_ref[at, :] = (grid[1, pl.ds(2 * r, 2)].reshape(2 * cols, width).astype(F32) * valid).astype(BF16)
         pre = pre_ref[at, :]
-        xin = s_ref[1, pl.ds(pl.multiple_of((r + 1) * cols, cols), cols), :].astype(F32)
+        xin = s_ref[1, pl.ds(pl.multiple_of((2 * r + 1) * cols, cols), 2 * cols), :].astype(F32)
         hidden = (valid * (xin + pre * jax.nn.sigmoid(pre))).astype(BF16)
         hid_ref[at, :] = hidden
         hidden = hidden.astype(F32)
         centred = hidden - jnp.mean(hidden, axis=-1, keepdims=True)
         spread = jnp.mean(centred * centred, axis=-1, keepdims=True)
-        norm_ref[at, :] = (centred * lax.rsqrt(spread + 1e-05) * gain_ref[...]).astype(BF16)
+        norm_ref[at, :] = (centred * lax.rsqrt(spread + 1e-05) * gain).astype(BF16)
         return carry
 
-    lax.fori_loop(0, rows, finish, 0)
+    lax.fori_loop(0, rows // 2, finish, 0)
     for group in ups + acrosses:
         for copy in group:
             copy.wait_send()
 
 
-def front(features, out_grad, conv_weight, valid, gain):
+def front(features, out_grad, conv_weight, ids, sizes, gain):
     count_y, count_x = lax.axis_size("sy"), lax.axis_size("sx")
     rows_dev, cols_dev, width = features.shape
     rows, cols = rows_dev * count_y, cols_dev * count_x
     cells = rows * cols
     vmem = pl.BlockSpec(memory_space=pltpu.VMEM)
     anywhere = pl.BlockSpec(memory_space=pl.ANY)
+    smem = pl.BlockSpec(memory_space=pltpu.SMEM)
     dma = pltpu.SemaphoreType.DMA
     return pl.pallas_call(
         front_kernel,
-        in_specs=[anywhere, anywhere, anywhere, vmem, vmem],
-        out_specs=[vmem] * 5,
+        in_specs=[anywhere, anywhere, anywhere, smem, smem, vmem],
+        out_specs=[vmem] * 6,
         out_shape=[
             jax.ShapeDtypeStruct((3, cells + 2 * cols, width), BF16),
             jax.ShapeDtypeStruct((cells, width), BF16),
             jax.ShapeDtypeStruct((cells, width), F32),
             jax.ShapeDtypeStruct((cells, width), BF16),
             jax.ShapeDtypeStruct((cells, width), BF16),
+            jax.ShapeDtypeStruct((cells, 1), F32),
         ],
         scratch_shapes=[
             pltpu.VMEM((2, rows, cols, width), BF16),
@@ -223,14 +257,14 @@
         compiler_params=pltpu.CompilerParams(
             collective_id=1, has_side_effects=True, vmem_limit_bytes=VMEM_LIMIT
         ),
-    )(features, out_grad, conv_weight, valid, gain)
+    )(features, out_grad, conv_weight, ids, sizes, gain)
 
 
 def back_kernel(
-    share, sq_ref, dq_ref, dk_ref, dv_ref, wq_ref, wk_ref, wv_ref, wo_ref,
+    share, n_ref, dq_ref, dk_ref, dv_ref, wq_ref, wk_ref, wv_ref, wo_ref,
     gb_ref, hid_ref, pre_ref, ctx_ref, valid_ref, gain_ref, s_ref,
-    cv_out, sq_out, block_out,
-    own, own_t, taps, cv, cv_pair, sq_pair, cv_sum, sq_sum, cv_got, sq_got,
+    cv_out, gq_out, gk_out, gv_out, go_out, block_out,
+    sq_ref, own, own_t, taps, cv, cv_pair, sq_pair, cv_sum, sq_sum, cv_got, sq_got,
     pair_send, pair_recv, far_send, far_recv,
 ):
     count = lax.axis_size("dp")
@@ -288,14 +322,29 @@
             copies[step].start()
         return copies
 
-    def collect(near, far, src, got, landed, out):
+    def collect(near, far, src, got, landed):
         near[0].wait_recv()
         value = src[me].astype(F32) + got[0].astype(F32)
         for step in order[:-1]:
             far[step].wait_recv()
             value += landed[step - 1].astype(F32)
-        out[...] = value
-
+        return value
+
+    def own_columns(value):
+        mine = value[:, 0:share]
+        for index in range(1, width // share):
+            mine = jnp.where(place == index, value[:, index * share : (index + 1) * share], mine)
+        return mine
+
+    dthree = [own_columns(ref[...]) for ref in (dq_ref, dk_ref, dv_ref)]
+    normed_t = n_ref[...].T
+    context_t = ctx_ref[...].reshape(cells, width).T
+    made = [jnp.dot(normed_t, part, preferred_element_type=F32) for part in dthree]
+    made.append(jnp.dot(context_t, own_columns(gb_ref[...]), preferred_element_type=F32))
+    made = jnp.concatenate(made, axis=1)
+    lines = width // count
+    for index in range(count):
+        sq_ref[index] = made[index * lines : (index + 1) * lines].astype(BF16)
     sq_near = to_partner(0, sq_ref, sq_pair)
 
     rows_at = cells // 4
@@ -310,17 +359,14 @@
         spread = jnp.mean(centred * centred, axis=-1, keepdims=True)
         rstd = lax.rsqrt(spread + 1e-05)
         unit = centred * rstd
-        up = dnormed * gain_ref[...]
+        up = dnormed * gain_ref[...].reshape(1, width)
         down = up - jnp.mean(up, axis=-1, keepdims=True)
         down = rstd * (down - unit * jnp.mean(up * unit, axis=-1, keepdims=True))
         pre = pre_ref[at, :]
         sig = jax.nn.sigmoid(pre)
         dpre = (gb_ref[at, :].astype(F32) + down) * sig * (1.0 + pre * (1.0 - sig))
         dpre = dpre * valid_ref[at, :]
-        mine = dpre[:, 0:share]
-        for index in range(1, width // share):
-            mine = jnp.where(place == index, dpre[:, index * share : (index + 1) * share], mine)
-        own[at, :] = mine
+        own[at, :] = own_columns(dpre)
         return carry
 
     lax.fori_loop(0, 4, backward, 0)
@@ -352,31 +398,34 @@
         block_out[r] = (value * valid_ref[line, :]).astype(BF16)
 
     cv_far = to_far(1, cv_near, cv, cv_pair, cv_sum, cv_got)
-    collect(sq_near, sq_far, sq_ref, sq_pair, sq_got, sq_out)
-    collect(cv_near, cv_far, cv, cv_pair, cv_got, cv_out)
+    squares = collect(sq_near, sq_far, sq_ref, sq_pair, sq_got)
+    for index, ref in enumerate((gq_out, gk_out, gv_out, go_out)):
+        ref[...] = squares[:, index * share : (index + 1) * share]
+    cv_out[...] = collect(cv_near, cv_far, cv, cv_pair, cv_got)[:, :piece].T
     for group in (sq_near, sq_far, cv_near, cv_far):
         for copy in group.values():
             copy.wait_send()
 
 
-def back(share, tile_shape, squares, arrays, context_grid, valid, gain, stack, piece):
-    count = squares.shape[0]
+def back(share, tile_shape, normed, arrays, context_grid, valid, gain, stack, piece):
+    count = lax.axis_size("dp")
     half = count // 2
     cells, width = arrays[0].shape
     lanes = -(-piece // 128) * 128
     vmem = pl.BlockSpec(memory_space=pltpu.VMEM)
     dma = pltpu.SemaphoreType.DMA
-    conv_shape, square_shape = (share, lanes), squares.shape[1:]
+    conv_shape, square_shape = (share, lanes), (width // count, 4 * share)
     return pl.pallas_call(
         functools.partial(back_kernel, share),
         in_specs=[vmem] * 15,
-        out_specs=[vmem] * 3,
+        out_specs=[vmem] * 6,
         out_shape=[
-            jax.ShapeDtypeStruct(conv_shape, F32),
-            jax.ShapeDtypeStruct(square_shape, F32),
+            jax.ShapeDtypeStruct((piece, share), F32),
+            *[jax.ShapeDtypeStruct((width // count, share), F32)] * 4,
             jax.ShapeDtypeStruct(tile_shape, BF16),
         ],
         scratch_shapes=[
+            pltpu.VMEM((count,) + square_shape, BF16),
             pltpu.VMEM((cells, share), F32),
             pltpu.VMEM((share, cells), BF16),
             pltpu.VMEM((share, 9 * width), F32),
@@ -395,7 +444,7 @@
         compiler_params=pltpu.CompilerParams(
             collective_id=2, has_side_effects=True, vmem_limit_bytes=VMEM_LIMIT
         ),
-    )(squares, *arrays, context_grid, valid, gain, stack)
+    )(normed, *arrays, context_grid, valid, gain, stack)
 
 
 def body(
@@ -414,57 +463,28 @@
     count_y = lax.axis_size("sy")
     count_x = lax.axis_size("sx")
     count_d = lax.axis_size("dp")
-    at_y, at_x = lax.axis_index("sy"), lax.axis_index("sx")
     rows, cols = rows_dev * count_y, cols_dev * count_x
-    cells = rows * cols
     share = width // (count_y * count_x)
-    first = (at_y * count_x + at_x) * share
-    chosen = jnp.arange(bucket_sizes.shape[0], dtype=jnp.int32) == bucket_ids[0]
-    height = jnp.sum(jnp.where(chosen, bucket_sizes[:, 0], 0))
-    breadth = jnp.sum(jnp.where(chosen, bucket_sizes[:, 1], 0))
-    valid = (jnp.arange(rows, dtype=jnp.int32)[:, None] < height) & (
-        jnp.arange(cols, dtype=jnp.int32)[None, :] < breadth
+    piece = conv_weight.shape[0] // count_d
+    stack, grad_b, pre, hidden, normed, valid = front(
+        features[0], out_grad[0], conv_weight, bucket_ids, bucket_sizes, norm_gain
     )
-    valid_flat = valid.reshape(-1, 1).astype(F32)
-    gain = norm_gain.reshape(1, width)
-
-    stack, grad_b, pre, hidden, normed = front(
-        features[0], out_grad[0], conv_weight, valid_flat, gain
+    weights = (query_weight, key_weight, value_weight, out_weight)
+    context, dquery, dkey, dvalue = attention(
+        bucket_ids, bucket_sizes, normed, grad_b, weights, HEADS, cols
     )
-    query = jnp.dot(normed, query_weight, preferred_element_type=F32).astype(BF16)
-    keys = jnp.dot(normed, key_weight, preferred_element_type=F32).astype(BF16)
-    values = jnp.dot(normed, value_weight, preferred_element_type=F32).astype(BF16)
-    grad_context = dot_t(grad_b, out_weight, 1, 1).astype(BF16)
-    context, dquery, dkey, dvalue = attention(
-        valid_flat.reshape(1, cells), query, keys, values, grad_context, HEADS
-    )
-
-    def own_columns(array):
-        return lax.dynamic_slice_in_dim(array, first, share, axis=1)
-
-    dthree = jnp.concatenate(
-        [own_columns(dquery), own_columns(dkey), own_columns(dvalue)], axis=1
-    )
-    squares = jnp.concatenate(
-        [dot_t(normed, dthree, 0, 0), dot_t(context, own_columns(grad_b), 0, 0)], axis=1
-    ).astype(BF16)
-    squares = squares.reshape(count_d, width // count_d, 4 * share)
-    piece = conv_weight.shape[0] // count_d
-    conv_sum, square_sum, block = back(
+    *grads, block = back(
         share,
         features.shape[1:],
-        squares,
-        (dquery, dkey, dvalue, query_weight, key_weight, value_weight, out_weight,
-         grad_b, hidden, pre),
+        normed,
+        (dquery, dkey, dvalue, *weights, grad_b, hidden, pre),
         context.reshape(rows, cols, width),
-        valid_flat,
-        gain,
+        valid,
+        norm_gain,
         stack,
         piece,
     )
-    grad_cv = conv_sum[:, :piece].T
-    grads = [square_sum[:, i * share : (i + 1) * share] for i in range(4)]
-    return (block[None], grad_cv, *grads)
+    return (block[None], *grads)
 
 
 def solution(mesh):

time: 115 us -> 107 us (0.930)
  matrix products: 9.96 us -> 0 us
  other arithmetic: 3.89 us -> 0 us
  local copies, waits for them, and re-layouts: 13.1 us -> 16.8 us
  Pallas kernels: 84.8 us -> 88.2 us
    unnamed x31 -> x25, local copies, waits for them, and re-layouts: 5.13 us -> 16.8 us
    dot_general x6 -> x0, matrix products: 9.96 us -> none  [the longest x3 4.83 us: dot_t(): lax.dot_general(a, b, (((ca,), (cb,)), ((), ())), preferred_element_type=...]
    pallas_call x1, Pallas kernels: 47.1 us -> 49.4 us  [back(): pl.pallas_call(functools.partial(back_kernel, share), in_specs=[vmem] * 1...]
    transpose x1 -> x0, local copies, waits for them, and re-layouts: 1.88 us -> none  [body(): grad_cv = conv_sum[:, :piece].T]
    slice x1 -> x0, local copies, waits for them, and re-layouts: 1.85 us -> none  [body(): grads = [square_sum[:, i * share:(i + 1) * share] for i in range(4)]]
    another operation x2 -> x0, local copies, waits for them, and re-layouts: 1.49 us -> none
    reduce_sum x1 -> x0, other arithmetic: 1.4 us -> none  [body(): height = jnp.sum(jnp.where(chosen, bucket_sizes[:, 0], 0))]
    lt x2 -> x0, other arithmetic: 1.3 us -> none  [the longest x1 0.65 us: body(): jnp.arange(rows, dtype=jnp.int32)[:, None] < height]
where the time goes in v3:
time: 107 us; the launch traced here: 106 us
  Pallas kernels  88.2 us (82%)
  local copies, waits for them, and re-layouts  16.8 us (16%)
  between operations  1.35 us (1%)
    pallas_call x1, Pallas kernels, back(): pl.pallas_call(functools.partial(back_kernel, share), in_specs=[vmem] * 1...  49.4 us
    pallas_call x1, Pallas kernels, front(): pl.pallas_call(front_kernel, in_specs=[anywhere, anywhere, anywhere, smem...  21.5 us
    pallas_call x1, Pallas kernels, attention(): pl.pallas_call(functools.partial(attention_kernel, width, cols), grid=(he...  17.3 us
    unnamed x25, local copies, waits for them, and re-layouts  16.8 us

profile of v3, /device:TPU:24, one launch (start us, length us, event | category | flops | bytes accessed | tf_op | source)
XLA Modules:
  0.0 106.3 jit_solution(350560412882644840)
XLA Ops:
  1.3 1.3 %copy.16.sizes_ref = s32[8,2]{1,0:T(8,128)} copy(s32[8,2]{0,1:T(2,128)} %param.12) | data formatting | bytes 128 | tf_op args[2]
  2.6 0.0 copy-start
  2.6 0.0 copy-start.1
  2.6 21.5 %shard_map.145 = (bf16[3,576,640]{2,1,0:T(8,128)(2,1)}, bf16[512,640]{1,0:T(8,128)(2,1)}, f32[512,640]{1,0:T(8,128)}, bf16[512,640]{1,0:T(8,128)(2,1)}, bf16[512,640]{1,0:T(8,128)(2,1)}, /*index=5*/f32[512,1]{1,0:T(8,128)}) custom-call(bf16[8,16,640]{2,1,0:T(8,128)(2,1)} %bitcast.6, bf16[8,16,640]{2,1,0:T(8,128)(2,1)} %bitcast.7, bf16[5760,640]{1,0:T(8,128)(2,1)} %w_ref.1, ...), custom_call_target="tpu_custom_call" | custom-call | tf_op jit(solution)/shard_map/pallas_call | solution.py:235
  24.1 0.0 copy-done
  24.1 0.0 copy-done.1
  24.1 0.0 copy-done.8
  24.1 0.0 copy-start.2
  24.1 1.1 %copy-done.2 = bf16[512,640]{1,0:T(8,128)(2,1)S(1)} copy-done((bf16[512,640]{1,0:T(8,128)(2,1)S(1)}, bf16[512,640]{1,0:T(8,128)(2,1)}, u32[]{:S(2)}) %copy-start.2) | copy-done | bytes 655384
  25.2 0.0 copy-start.3
  25.2 1.1 %copy-done.3 = bf16[512,640]{1,0:T(8,128)(2,1)S(1)} copy-done((bf16[512,640]{1,0:T(8,128)(2,1)S(1)}, bf16[512,640]{1,0:T(8,128)(2,1)}, u32[]{:S(2)}) %copy-start.3) | copy-done | bytes 655384
  26.3 17.3 %shard_map.146 = (bf16[512,640]{1,0:T(8,128)(2,1)S(1)}, bf16[512,640]{1,0:T(8,128)(2,1)S(1)}, bf16[512,640]{1,0:T(8,128)(2,1)S(1)}, bf16[512,640]{1,0:T(8,128)(2,1)S(1)}) custom-call(s32[1]{0:T(128)S(6)} %copy.24.ids_ref, s32[8,2]{1,0:T(8,128)S(1)} %copy-done.8, bf16[512,640]{1,0:T(8,128)(2,1)S(1)} %copy-done.3, bf16[512,640]{1,0:T(8,128)(2,1)S(1)} %copy-done.2, ...), custom_call_target="tpu_custom_call" | custom-call | flops 3690987520 | bytes 5242880 | tf_op jit(solution)/shard_map/pallas_call | solution.py:73
  43.6 0.0 copy-start.4
  43.6 0.9 copy-done.4
  44.5 0.8 copy-done.5
  45.4 0.8 copy-done.6
  46.2 0.8 copy-done.7
  47.1 49.4 %shard_map.147 = (f32[720,160]{1,0:T(8,128)}, f32[80,160]{1,0:T(8,128)}, f32[80,160]{1,0:T(8,128)}, f32[80,160]{1,0:T(8,128)}, f32[80,160]{1,0:T(8,128)}, /*index=5*/bf16[8,16,640]{2,1,0:T(8,128)(2,1)}) custom-call(bf16[512,640]{1,0:T(8,128)(2,1)} %get-tuple-element.22.n_ref, bf16[512,640]{1,0:T(8,128)(2,1)} %copy-done.5, bf16[512,640]{1,0:T(8,128)(2,1)} %copy-done.6, ...), custom_call_target="tpu_custom_call" | custom-call | tf_op jit(solution)/shard_map/pallas_call | solution.py:418
  96.5 2.1 %copy.18 = f32[720,160]{0,1:T(8,128)} copy(f32[720,160]{1,0:T(8,128)} %get-tuple-element.39) | data formatting | bytes 921600
  98.6 1.6 %copy.25 = bf16[1,8,16,640]{3,2,1,0:T(8,128)(2,1)} copy(bf16[1,8,16,640]{3,2,1,0:T(8,128)(2,1)} %bitcast.5) | data formatting | bytes 327680
  100.2 1.5 %copy.26 = f32[80,160]{1,0:T(8,128)} copy(f32[80,160]{1,0:T(8,128)} %get-tuple-element.52) | data formatting | bytes 102400
  101.7 1.5 %copy.27 = f32[80,160]{1,0:T(8,128)} copy(f32[80,160]{1,0:T(8,128)} %get-tuple-element.53) | data formatting | bytes 102400
  103.3 1.5 %copy.28 = f32[80,160]{1,0:T(8,128)} copy(f32[80,160]{1,0:T(8,128)} %get-tuple-element.54) | data formatting | bytes 102400
  104.8 1.5 %copy.29 = f32[80,160]{1,0:T(8,128)} copy(f32[80,160]{1,0:T(8,128)} %get-tuple-element.55) | data formatting | bytes 102400
  (4 shorter events, 0.0 us)
Async XLA Ops:
  2.6 21.5 %copy-start = (bf16[640,640]{1,0:T(8,128)(2,1)S(1)}, bf16[640,640]{1,0:T(8,128)(2,1)}, u32[]{:S(2)}) copy-start(bf16[640,640]{1,0:T(8,128)(2,1)} %wq_ref.3) | copy-start | bytes 2457604
  2.6 21.5 %copy-start.1 = (bf16[640,640]{1,0:T(8,128)(2,1)S(1)}, bf16[640,640]{1,0:T(8,128)(2,1)}, u32[]{:S(2)}) copy-start(bf16[640,640]{1,0:T(8,128)(2,1)} %wk_ref.3) | copy-start | bytes 2457604
  2.6 21.5 %copy-start.8 = (s32[8,2]{1,0:T(8,128)S(1)}, s32[8,2]{1,0:T(8,128)}, u32[]{:S(2)}) copy-start(s32[8,2]{1,0:T(8,128)} %copy.16.sizes_ref) | copy-start | bytes 196
  24.1 1.1 %copy-start.2 = (bf16[512,640]{1,0:T(8,128)(2,1)S(1)}, bf16[512,640]{1,0:T(8,128)(2,1)}, u32[]{:S(2)}) copy-start(bf16[512,640]{1,0:T(8,128)(2,1)} %get-tuple-element.23.gb_ref) | copy-start | bytes 1966084
  25.2 1.1 %copy-start.3 = (bf16[512,640]{1,0:T(8,128)(2,1)S(1)}, bf16[512,640]{1,0:T(8,128)(2,1)}, u32[]{:S(2)}) copy-start(bf16[512,640]{1,0:T(8,128)(2,1)} %get-tuple-element.22.n_ref) | copy-start | bytes 1966084
  43.6 0.9 copy-start.4
  44.5 0.8 copy-start.5
  45.4 0.8 copy-start.6
  46.2 0.8 copy-start.7
